TPU v7x, 32 devices: a whole 2x2x4 slice. The times are simulated.
32 devices in a mesh: group: 2 (over x), tensor: 8 (over z, y), replica: 2 (over core).
Axes of the slice: x: 2, y: 2, z: 4, core: 2. Of those that a mesh axis runs over, the one named last changes fastest.
Arguments:
- hidden_in: bfloat16 [2, 256, 8192], P(None, ('group', 'replica')), parts along dimension 1, may hold values from -6 to 6
- norm_gain: bfloat16 [8192], replicated, may hold values from 0.25 to 1.75
- w_query: bfloat16 [8192, 4096], P(None, 'tensor'), may hold values from -0.0625 to 0.0625
- w_keyval: bfloat16 [8192, 1024], P(None, 'tensor'), may hold values from -0.0625 to 0.0625
- w_out: bfloat16 [4096, 8192], P('tensor'), may hold values from -0.09375 to 0.09375
- cache_kv: bfloat16 [2, 256, 384, 1024], P(None, ('group', 'replica'), None, 'tensor'), parts along dimension 1
- cache_len: int32 [256], P(('group', 'replica')), parts along dimension 0, may hold values from 1 to 384
- prompt_kv: bfloat16 [2, 64, 256, 512], P(None, ('group', 'tensor', 'replica')), parts along dimension 1
- block_count: int32 [64], P('group'), parts along dimension 0, may hold values from 1 to 4
- slot_of: int32 [64], P('group'), parts along dimension 0, may hold values from 0 to 127, as said below
Outputs:
- attended: bfloat16 [2, 256, 8192], P(None, ('group', 'replica'), 'tensor'), parts along dimension 1
There are 2 independent parts, one for each index of `group`. A program takes and returns all parts, laid end to end along the dimension named above; an argument that names none is the same for every part. Nothing has to cross between parts.
Inputs may be any that keep to these rules, and one draw needn't show every extreme that they name: `slot_of`: distinct slots; slot 0 and slot 127 are always taken.
All inputs are finite; a program needn't handle non-finite values.
Results may differ from a plain program's by a relative error of at most 0.012.
The roundings to bfloat16 on the way count: a program that leaves them out, or rounds other values in their place, can miss the bound.
Values may be sent and summed in bfloat16 or wider, within the bound.
A program may use at most 128 MiB of HBM per device.

v0:
```python
import jax
import jax.numpy as jnp
from jax import lax
from jax.sharding import PartitionSpec as P

KVH = 4
HD = 128
GROUP = 8
BLOCK = 64


EPSILON = 1e-05
THETA = 500000.0
NEGATIVE = -1e30


def rotate(values, positions):
    half_dim = values.shape[-1] // 2
    freqs = THETA ** (-2.0 * jnp.arange(half_dim, dtype=jnp.float32) / values.shape[-1])
    angles = positions[..., None].astype(jnp.float32) * freqs
    cosine = jnp.cos(angles)
    sine = jnp.sin(angles)
    first = values[..., :half_dim]
    second = values[..., half_dim:]
    return jnp.concatenate([first * cosine - second * sine, second * cosine + first * sine], -1)


def attend(
    queries,
    cache_keys,
    cache_values,
    prompt_keys,
    prompt_values,
    new_keys,
    new_values,
    cache_valid,
    prompt_valid,
    own_valid,
):
    scaling = HD ** (-0.5)
    score_cache = (
        jnp.einsum("jshd,scd->jshc", queries, cache_keys, preferred_element_type=jnp.float32)
        * scaling
    )
    score_prompt = (
        jnp.einsum("jshd,spd->jshp", queries, prompt_keys, preferred_element_type=jnp.float32)
        * scaling
    )
    score_own = (
        jnp.einsum("jshd,isd->jshi", queries, new_keys, preferred_element_type=jnp.float32)
        * scaling
    )
    score_cache = jnp.where(cache_valid[None, :, None, :], score_cache, NEGATIVE)
    score_prompt = jnp.where(prompt_valid[None, :, None, :], score_prompt, NEGATIVE)
    score_own = jnp.where(own_valid[:, None, None, :], score_own, NEGATIVE)
    top = jnp.maximum(
        jnp.maximum(jnp.max(score_cache, -1), jnp.max(score_prompt, -1)), jnp.max(score_own, -1)
    )[..., None]
    exp_cache = jnp.exp(score_cache - top)
    exp_prompt = jnp.exp(score_prompt - top)
    exp_own = jnp.exp(score_own - top)
    summed = (jnp.sum(exp_cache, -1) + jnp.sum(exp_prompt, -1) + jnp.sum(exp_own, -1))[..., None]
    weight_cache = (exp_cache / summed).astype(jnp.bfloat16)
    weight_prompt = (exp_prompt / summed).astype(jnp.bfloat16)
    weight_own = (exp_own / summed).astype(jnp.bfloat16)
    result = jnp.einsum(
        "jshc,scd->jshd", weight_cache, cache_values, preferred_element_type=jnp.float32
    )
    result = result + jnp.einsum(
        "jshp,spd->jshd", weight_prompt, prompt_values, preferred_element_type=jnp.float32
    )
    result = result + jnp.einsum(
        "jshi,isd->jshd", weight_own, new_values, preferred_element_type=jnp.float32
    )
    return result.astype(jnp.bfloat16)


def local(
    hidden_in,
    norm_gain,
    w_query,
    w_keyval,
    w_out,
    cache_kv,
    cache_len,
    prompt_kv,
    block_count,
    slot_of,
):
    tensor_size = lax.axis_size("tensor")
    replica_size = lax.axis_size("replica")
    tensor_rank = lax.axis_index("tensor")
    replica_rank = lax.axis_index("replica")
    step_count, row_count, model_width = hidden_in.shape
    local_heads = w_query.shape[1] // HD
    kv_head = tensor_rank * local_heads // GROUP
    per_device = prompt_kv.shape[1]
    prompt_cap = prompt_kv.shape[2]
    capacity = cache_kv.shape[2]
    hidden = hidden_in.astype(jnp.float32)
    scale = lax.rsqrt(jnp.mean(hidden * hidden, -1, keepdims=True) + EPSILON)
    normed = (hidden * scale * norm_gain.astype(jnp.float32)).astype(jnp.bfloat16)
    flat = normed.reshape(step_count * row_count, model_width)
    queries = jnp.dot(flat, w_query, preferred_element_type=jnp.float32).reshape(
        step_count, row_count, local_heads, HD
    )
    keyval_part = jnp.dot(flat, w_keyval, preferred_element_type=jnp.float32).astype(jnp.bfloat16)
    keyval_part = keyval_part.reshape(step_count, row_count, -1)
    keyval = lax.all_gather(keyval_part, "tensor", axis=2, tiled=True).reshape(
        step_count, row_count, 2, KVH, HD
    )
    own_pair = lax.dynamic_index_in_dim(keyval, kv_head, 3, keepdims=False)
    slot_ids = replica_rank * row_count + jnp.arange(row_count, dtype=jnp.int32)
    matches = slot_of[None, :] == slot_ids[:, None]
    matched = jnp.any(matches, 1)
    request_count = slot_of.shape[0]
    request = jnp.sum(jnp.where(matches, jnp.arange(request_count, dtype=jnp.int32)[None, :], 0), 1)
    prompt_len = jnp.sum(jnp.where(matches, block_count[None, :], 0), 1) * BLOCK
    base_pos = jnp.where(matched, prompt_len, cache_len)
    positions = base_pos[None, :] + jnp.arange(step_count, dtype=jnp.int32)[:, None]
    queries = rotate(queries, positions[:, :, None]).astype(jnp.bfloat16)
    new_keys = rotate(own_pair[:, :, 0].astype(jnp.float32), positions).astype(jnp.bfloat16)
    new_values = own_pair[:, :, 1]
    everything = lax.all_gather(prompt_kv, "tensor", axis=1, tiled=True)
    own_prompts = lax.dynamic_slice_in_dim(everything, kv_head * HD, HD, 3)
    paired = lax.all_gather(own_prompts, "replica", axis=1, tiled=True)
    sender = request // per_device
    within = request % per_device
    sender_tensor = sender // replica_size
    sender_replica = sender % replica_size
    position = (sender_replica * tensor_size + sender_tensor) * per_device + within
    chosen = jnp.take(paired, position, axis=1)
    cache_valid = jnp.logical_not(matched)[:, None] & (
        jnp.arange(capacity, dtype=jnp.int32)[None, :] < cache_len[:, None]
    )
    prompt_valid = matched[:, None] & (
        jnp.arange(prompt_cap, dtype=jnp.int32)[None, :] < prompt_len[:, None]
    )
    own_valid = (
        jnp.arange(step_count, dtype=jnp.int32)[None, :]
        <= jnp.arange(step_count, dtype=jnp.int32)[:, None]
    )
    heads_out = attend(
        queries,
        cache_kv[0],
        cache_kv[1],
        chosen[0],
        chosen[1],
        new_keys,
        new_values,
        cache_valid,
        prompt_valid,
        own_valid,
    )
    heads_flat = heads_out.reshape(step_count * row_count, local_heads * HD)
    partial_sums = jnp.dot(heads_flat, w_out, preferred_element_type=jnp.float32).reshape(
        step_count, row_count, model_width
    )
    totals = lax.psum(partial_sums, "tensor")
    share_width = model_width // tensor_size
    return lax.dynamic_slice_in_dim(totals, tensor_rank * share_width, share_width, 2).astype(
        jnp.bfloat16
    )


def solution(mesh):
    in_specs = (
        P(None, ("group", "replica"), None),
        P(),
        P(None, "tensor"),
        P(None, "tensor"),
        P("tensor", None),
        P(None, ("group", "replica"), None, "tensor"),
        P(("group", "replica")),
        P(None, ("group", "tensor", "replica"), None, None),
        P("group"),
        P("group"),
    )
    out_specs = P(None, ("group", "replica"), "tensor")
    return jax.shard_map(local, mesh=mesh, in_specs=in_specs, out_specs=out_specs, check_vma=False)
```

profile of v0, /device:TPU:0, one launch (start us, length us, event | category | flops | bytes accessed | tf_op | source)
XLA Modules:
  0.0 377.6 jit_solution(8085096198251737059)
XLA Ops:
  6.5 0.0 copy-start
  6.5 0.0 all-gather.3.cloned.1.call-start
  6.5 0.7 all-gather.3.cloned.1.call-update
  7.3 0.0 all-gather.5.cloned.1.call-start
  7.3 0.7 convert_element_type.50
  8.0 2.1 fusion.9
  10.2 0.0 copy-start.5
  10.2 2.2 fusion.11
  12.4 0.0 copy-start.2
  12.4 1.3 copy-done.2
  13.7 0.0 copy-done
  13.7 0.7 convolution_convert_fusion
  14.4 29.7 %all_gather.11 = bf16[2,64,1024]{2,1,0:T(8,128)(2,1)S(1)} all-gather(bf16[2,64,128]{2,1,0:T(8,128)(2,1)S(1)} %bitcast.141), channel_id=1, replica_groups=mesh['group'=2,'tensor'=8,'replica'=2] {'tensor'}, dimensions={2}, use_global_device_ids=true | all-gather | bytes 294912 | tf_op jit(solution)/shard_map/all_gather | solution.py:109
  44.2 0.2 reshape.345
  44.4 0.0 copy-done.5
  44.4 0.1 compare_reduce_fusion
  44.5 0.1 constant_dynamic-slice_fusion
  44.6 96.3 %all-gather.3.cloned.1.call-done = bf16[2,16,256,512]{3,2,1,0:T(8,128)(2,1)} async-done(((bf16[2,2,256,512]{3,2,1,0:T(8,128)(2,1)}), bf16[2,16,256,512]{3,2,1,0:T(8,128)(2,1)}) %all-gather.3.cloned.1.call-update) | async-done | bytes 8388624 | tf_op jit(solution)/shard_map/all_gather | solution.py:124
  140.9 3.2 constant_dynamic-slice_fusion.1
  144.1 0.0 all-gather.5.cloned.1.call-update
  144.1 0.0 copy-start.6
  144.1 0.0 copy-start.4
  144.2 0.0 copy-start.3
  144.2 12.3 %copy.61 = bf16[512,8192]{1,0:T(8,128)(2,1)} copy(bf16[512,8192]{0,1:T(8,128)(2,1)} %bitcast.130) | data formatting | bytes 16777216 | tf_op jit(solution)/shard_map/dot_general | solution.py:104
  156.5 0.0 copy-done.6
  156.5 0.1 fusion.56
  156.7 0.0 copy-done.4
  156.7 0.3 subtract_convert_fusion.1
  157.1 0.1 maximum_bitcast_fusion
  157.2 0.0 copy-done.3
  157.2 6.3 %fusion.14 = f32[2,64,4,128]{3,1,2,0:T(8,128)S(1)} fusion(bf16[4,128,8192,1]{2,1,0,3:T(8,128)(2,1)} %bitcast.126, bf16[2,64,8192]{2,1,0:T(8,128)(2,1)S(1)} %copy-done.3), kind=kOutput, calls=%fused_computation.20 | convolution fusion | flops 1073741824 | bytes 10747904 | tf_op jit(solution)/shard_map/dot_general | solution.py:104
  163.5 0.2 subtract_convert_fusion
  163.6 0.1 pad_maximum_fusion
  163.8 0.1 fusion.51
  163.9 0.1 fusion.44
  164.0 1.3 fusion.65
  165.3 5.2 %fusion.66 = (f32[2,64,4]{2,0,1:T(2,128)S(1)}, f32[2,64,4,384]{3,2,0,1:T(4,128)S(1)}) fusion(bf16[2,64,384,128]{3,2,1,0:T(8,128)(2,1)} %param.15, bf16[2,64,4,128]{3,1,2,0:T(8,128)(2,1)S(1)} %pad_maximum_fusion, pred[64,384]{1,0:T(8,128)(4,1)S(1)} %fusion.44), kind=kOutput, calls=%fused_computation.125 | convolution fusion | flops 50920960 | bytes 7235584 | tf_op jit(solution)/shard_map/jshd,scd->jshc/dot_general | solution.py:42
  170.5 0.0 all-gather.5.cloned.1.call-done
  170.5 7.5 %gather_fusion = bf16[64,2,256,128]{3,2,1,0:T(8,128)(2,1)} fusion(bf16[2,32,256,128]{3,2,1,0:T(8,128)(2,1)} %all-gather.5.cloned.1.call-done, s32[1024]{0:T(1024)S(1)} %pad_clamp_fusion), kind=kCustom, calls=%fused_computation | custom fusion | bytes 16777472 | tf_op jit(solution)/shard_map/jit(_take)/gather | solution.py:132
  178.0 7.5 %fusion.2 = bf16[2,64,256,128]{3,2,1,0:T(8,128)(2,1)} fusion(bf16[64,2,256,128]{3,2,1,0:T(8,128)(2,1)} %gather_fusion, pred[64]{0:T(512)(128)(4,1)S(1)} %compare_and_fusion), kind=kLoop, calls=%fused_computation.4 | loop fusion | flops 4194304 | bytes 16777280 | tf_op jit(solution)/shard_map/jit(_take)/select_n | solution.py:132
  185.6 3.5 fusion.67
  189.1 0.3 fusion.45
  189.4 0.6 fusion.37
  189.9 0.0 slice-start
  190.0 0.4 fusion.38
  190.4 0.0 slice-start.1
  190.4 4.4 %fusion.20 = f32[2,64,4,128]{3,2,0,1:T(4,128)S(1)} fusion(bf16[2,64,384,128]{3,2,1,0:T(8,128)(2,1)} %param.15, f32[2,64,4,384]{3,2,0,1:T(4,128)S(1)} %get-tuple-element.20, f32[2,64,4]{2,0,1:T(2,128)S(1)} %bitcast.144, f32[2,64,4]{2,0,1:T(2,128)S(1)} %bitcast.134), kind=kOutput, calls=%fused_computation.24 | convolution fusion | flops 50921472 | bytes 7344128 | tf_op jit(solution)/shard_map/jshc,scd->jshd/dot_general | solution.py:66
  194.8 0.0 slice-done
  194.8 0.5 slice-done.1
  195.3 0.8 fusion.25
  196.2 0.4 fusion.26
  196.5 0.1 dot_general.43
  196.6 0.0 copy-start.1
  196.6 6.7 %fusion = f32[2,64,8192]{2,1,0:T(8,128)} fusion(bf16[512,8192]{1,0:T(8,128)(2,1)} %param.14, bf16[2,64,512]{2,0,1:T(2,128)(2,1)S(1)} %dot_general.43), kind=kOutput, calls=%fused_computation.1 | convolution fusion | flops 1073741824 | bytes 12713984 | tf_op jit(solution)/shard_map/dot_general | solution.py:156
  203.3 165.8 %all-reduce.1 = bf16[2,64,8192]{2,1,0:T(8,128)(2,1)} all-reduce(f32[2,64,8192]{2,1,0:T(8,128)} %fusion), channel_id=1, replica_groups=mesh['group'=2,'tensor'=8,'replica'=2] {'tensor'}, use_global_device_ids=true, to_apply=%region_10.11 | all-reduce | flops 1048576 | bytes 6291456 | tf_op jit(solution)/shard_map/psum | solution.py:159
  369.1 1.7 dynamic-slice_convert_fusion
  370.8 0.0 copy-done.1
  (15 shorter events, 0.2 us)
Async XLA Ops:
  6.5 7.2 %copy-start = (bf16[8192,128]{1,0:T(8,128)(2,1)S(1)}, bf16[8192,128]{1,0:T(8,128)(2,1)}, u32[]{:S(2)}) copy-start(bf16[8192,128]{1,0:T(8,128)(2,1)} %param.13) | copy-start | bytes 6291460
  6.5 134.4 %all-gather.3.cloned.1.call-start = ((), (), s32[]{:S(2)}) async-start(), calls=%async_computation | async-start | bytes 9437184 | tf_op jit(solution)/shard_map/all_gather | solution.py:124
  7.3 163.2 %all-gather.5.cloned.1.call-start = ((), (), s32[]{:S(2)}) async-start(), calls=%async_computation.1 | async-start | bytes 6291456 | tf_op jit(solution)/shard_map/all_gather | solution.py:126
  10.2 34.2 %copy-start.5 = (s32[32]{0:T(128)S(1)}, s32[32]{0:T(128)}, u32[]{:S(2)}) copy-start(s32[32]{0:T(128)} %param.19) | copy-start | bytes 388
  12.4 1.3 copy-start.2
  144.1 12.4 %copy-start.6 = (s32[32]{0:T(128)S(1)}, s32[32]{0:T(128)}, u32[]{:S(2)}) copy-start(s32[32]{0:T(128)} %param.18) | copy-start | bytes 388
  144.1 12.5 %copy-start.4 = (s32[64]{0:T(128)S(1)}, s32[64]{0:T(128)}, u32[]{:S(2)}) copy-start(s32[64]{0:T(128)} %param.16) | copy-start | bytes 772
  144.2 13.0 %copy-start.3 = (bf16[2,64,8192]{2,1,0:T(8,128)(2,1)S(1)}, bf16[2,64,8192]{2,1,0:T(8,128)(2,1)}, u32[]{:S(2)}) copy-start(bf16[2,64,8192]{2,1,0:T(8,128)(2,1)} %copy-done.2) | copy-start | bytes 6291460
  189.9 4.9 %slice-start = ((s8[8388608]{0:T(1024)(128)(4,1)}), s8[4194304]{0:T(1024)(128)(4,1)S(1)}, s32[]{:S(2)}) async-start(s8[8388608]{0:T(1024)(128)(4,1)} %bitcast.128), calls=%async_computation.2 | async-start | bytes 8388608
  190.4 4.9 %slice-start.1 = ((s8[8388608]{0:T(1024)(128)(4,1)}), s8[4194304]{0:T(1024)(128)(4,1)S(1)}, s32[]{:S(2)}) async-start(s8[8388608]{0:T(1024)(128)(4,1)} %bitcast.128), calls=%async_computation.3 | async-start | bytes 8388608
  196.6 174.2 %copy-start.1 = (bf16[8192,128]{1,0:T(8,128)(2,1)S(1)}, bf16[8192,128]{1,0:T(8,128)(2,1)}, u32[]{:S(2)}) copy-start(bf16[8192,128]{1,0:T(8,128)(2,1)} %param.13) | copy-start | bytes 6291460
Sparse Core Ops, SparseCore 0:
  9.5 131.3 all-gather.2
  144.2 11.8 all-gather.4
where the time goes:
time: 378 us
  blocking collectives  196 us (52%)
  waiting for transfers between devices  97 us (26%)
  matrix products  29.3 us (8%)
  local copies, waits for them, and re-layouts  27 us (7%)
  other arithmetic  15 us (4%)
  between operations  13.7 us (4%)
    psum x1, blocking collectives, local(): totals = lax.psum(partial_sums, 'tensor')  166 us
    all_gather x1, waiting for transfers between devices, local(): everything = lax.all_gather(prompt_kv, 'tensor', axis=1, tiled=True)  96.3 us
    all_gather x1, blocking collectives, local(): lax.all_gather(keyval_part, 'tensor', axis=2, tiled=True)  29.7 us
    dot_general x1, local copies, waits for them, and re-layouts, local(): jnp.dot(flat, w_query, preferred_element_type=jnp.float32)  12.3 us
    select_n x2, other arithmetic, local(): chosen = jnp.take(paired, position, axis=1)  7.57 us
  transfers between devices with their start and end apart: 2, of which 1 were waited for; matrix products, arithmetic and copies ran while one was open for 9% of the time, Pallas kernels for 0%

commit v1 on v0

--- a/solution.py
+++ b/solution.py
@@ -1,6 +1,10 @@
+import functools
+
 import jax
 import jax.numpy as jnp
 from jax import lax
+from jax.experimental import pallas as pl
+from jax.experimental.pallas import tpu as pltpu
 from jax.sharding import PartitionSpec as P
 
 KVH = 4
@@ -12,6 +16,91 @@
 EPSILON = 1e-05
 THETA = 500000.0
 NEGATIVE = -1e30
+MESH = pl.DeviceIdType.MESH
+
+
+def out_kernel(size, heads_ref, w_ref, out_ref, wbuf, own, send1, recv1, send2, recv2, wsem, s1s, s1r, s2s, s2r):
+    half = size // 2
+    rank = lax.axis_index("tensor")
+    mine = rank // 2
+    side = lax.rem(rank, 2)
+    partner = rank + 1 - 2 * side
+    width = out_ref.shape[1]
+    offsets = [o for o in range(half // 2, half)] + [o for o in range(1, half // 2)] + [0]
+
+    weights = []
+    for at, off in enumerate(offsets):
+        block = lax.rem(mine + off, half)
+        for which, target in enumerate((2 * block + 1 - side, 2 * block + side)):
+            columns = pl.ds(pl.multiple_of(target * width, 128), width)
+            copy = pltpu.make_async_copy(w_ref.at[:, columns], wbuf.at[at, which], wsem.at[at, which])
+            copy.start()
+            weights.append(copy)
+
+    barrier = pltpu.get_barrier_semaphore()
+    peers = [partner] + [2 * lax.rem(mine + off, half) + side for off in range(1, half)]
+    for peer in peers:
+        pl.semaphore_signal(barrier, inc=1, device_id={"tensor": peer}, device_id_type=MESH)
+    pl.semaphore_wait(barrier, len(peers))
+
+    heads = heads_ref[...]
+    first = []
+    for at in range(half):
+        weights[2 * at].wait()
+        send1[at] = jnp.dot(heads, wbuf[at, 0], preferred_element_type=jnp.float32).astype(jnp.bfloat16)
+        copy = pltpu.make_async_remote_copy(
+            src_ref=send1.at[at], dst_ref=recv1.at[at], send_sem=s1s.at[at], recv_sem=s1r.at[at],
+            device_id={"tensor": partner}, device_id_type=MESH)
+        copy.start()
+        first.append(copy)
+    for at in range(half):
+        weights[2 * at + 1].wait()
+        own[at] = jnp.dot(heads, wbuf[at, 1], preferred_element_type=jnp.float32)
+    second = []
+    for at, off in enumerate(offsets):
+        first[at].wait_recv()
+        total = own[at] + recv1[at].astype(jnp.float32)
+        if off != 0:
+            send2[at] = total.astype(jnp.bfloat16)
+            copy = pltpu.make_async_remote_copy(
+                src_ref=send2.at[at], dst_ref=recv2.at[at], send_sem=s2s.at[at], recv_sem=s2r.at[at],
+                device_id={"tensor": 2 * lax.rem(mine + off, half) + side}, device_id_type=MESH)
+            copy.start()
+            second.append(copy)
+        else:
+            own[at] = total
+    for at in range(half - 1):
+        second[at].wait_recv()
+        own[half - 1] += recv2[at].astype(jnp.float32)
+    out_ref[...] = own[half - 1].astype(jnp.bfloat16)
+    for copy in first + second:
+        copy.wait_send()
+
+
+def project_out(heads, w_out, size):
+    rows, depth = heads.shape
+    width = w_out.shape[1] // size
+    half = size // 2
+    return pl.pallas_call(
+        functools.partial(out_kernel, size),
+        out_shape=jax.ShapeDtypeStruct((rows, width), jnp.bfloat16),
+        in_specs=[pl.BlockSpec(memory_space=pltpu.VMEM), pl.BlockSpec(memory_space=pl.ANY)],
+        out_specs=pl.BlockSpec(memory_space=pltpu.VMEM),
+        scratch_shapes=[
+            pltpu.VMEM((half, 2, depth, width), jnp.bfloat16),
+            pltpu.VMEM((half, rows, width), jnp.float32),
+            pltpu.VMEM((half, rows, width), jnp.bfloat16),
+            pltpu.VMEM((half, rows, width), jnp.bfloat16),
+            pltpu.VMEM((half - 1, rows, width), jnp.bfloat16),
+            pltpu.VMEM((half - 1, rows, width), jnp.bfloat16),
+            pltpu.SemaphoreType.DMA((half, 2)),
+            pltpu.SemaphoreType.DMA((half,)),
+            pltpu.SemaphoreType.DMA((half,)),
+            pltpu.SemaphoreType.DMA((half - 1,)),
+            pltpu.SemaphoreType.DMA((half - 1,)),
+        ],
+        compiler_params=pltpu.CompilerParams(collective_id=1, has_side_effects=True, vmem_limit_bytes=40 * 2**20),
+    )(heads, w_out)
 
 
 def rotate(values, positions):
@@ -153,14 +242,8 @@
         own_valid,
     )
     heads_flat = heads_out.reshape(step_count * row_count, local_heads * HD)
-    partial_sums = jnp.dot(heads_flat, w_out, preferred_element_type=jnp.float32).reshape(
-        step_count, row_count, model_width
-    )
-    totals = lax.psum(partial_sums, "tensor")
-    share_width = model_width // tensor_size
-    return lax.dynamic_slice_in_dim(totals, tensor_rank * share_width, share_width, 2).astype(
-        jnp.bfloat16
-    )
+    mixed = project_out(heads_flat, w_out, tensor_size)
+    return mixed.reshape(step_count, row_count, -1)
 
 
 def solution(mesh):

time: 378 us -> 237 us (0.63)
  blocking collectives: 196 us -> 29.7 us
  Pallas kernels: 0 us -> 31.3 us
  matrix products: 29.3 us -> 22.6 us
    psum x1 -> x0, blocking collectives: 166 us -> none  [local(): totals = lax.psum(partial_sums, 'tensor')]
    pallas_call x0 -> x1, Pallas kernels: none -> 31.3 us  [project_out(): pl.pallas_call(functools.partial(out_kernel, size), out_shape=jax.ShapeDt...]
    dot_general x1 -> x0, matrix products: 6.72 us -> none  [local(): jnp.dot(heads_flat, w_out, preferred_element_type=jnp.float32)]
  transfers between devices with their start and end apart: 2 -> 2, of which waited for: 1 -> 1; matrix products, arithmetic and copies ran while one was open for 9% -> 14% of each run, Pallas kernels for 0% -> 0%
where the time goes in v1:
time: 237 us; the launch traced here: 236 us
  waiting for transfers between devices  97 us (41%)
  Pallas kernels  31.3 us (13%)
  blocking collectives  29.7 us (13%)
  local copies, waits for them, and re-layouts  26.7 us (11%)
  matrix products  22.6 us (10%)
  other arithmetic  15 us (6%)
  between operations  13.8 us (6%)
    all_gather x1, waiting for transfers between devices, local(): everything = lax.all_gather(prompt_kv, 'tensor', axis=1, tiled=True)  96.3 us
    pallas_call x1, Pallas kernels, project_out(): pl.pallas_call(functools.partial(out_kernel, size), out_shape=jax.ShapeDt...  31.3 us
    all_gather x1, blocking collectives, local(): lax.all_gather(keyval_part, 'tensor', axis=2, tiled=True)  29.7 us
    dot_general x1, local copies, waits for them, and re-layouts, local(): jnp.dot(flat, w_query, preferred_element_type=jnp.float32)  12.4 us
    select_n x2, other arithmetic, local(): chosen = jnp.take(paired, position, axis=1)  7.57 us
    gather x1, local copies, waits for them, and re-layouts, local(): chosen = jnp.take(paired, position, axis=1)  7.53 us
    dot_general x1, matrix products, local(): jnp.dot(flat, w_query, preferred_element_type=jnp.float32)  6.3 us
    dot_general x1, matrix products, attend(): jnp.einsum('jshd,scd->jshc', queries, cache_keys, preferred_element_type=...  5.18 us
  transfers between devices with their start and end apart: 2, of which 1 were waited for; matrix products, arithmetic and copies ran while one was open for 14% of the time, Pallas kernels for 0%

profile of v1, /device:TPU:0, one launch (start us, length us, event | category | flops | bytes accessed | tf_op | source)
XLA Modules:
  0.0 236.2 jit_solution(11207056848533731779)
XLA Ops:
  6.5 0.0 copy-start
  6.5 0.0 all-gather.3.cloned.1.call-start
  6.5 0.7 all-gather.3.cloned.1.call-update
  7.3 0.0 all-gather.5.cloned.1.call-start
  7.3 0.7 convert_element_type.47
  8.0 2.1 fusion.7
  10.2 0.0 copy-start.5
  10.2 2.2 fusion.9
  12.4 0.0 copy-start.2
  12.4 1.3 copy-done.2
  13.7 0.0 copy-done
  13.7 0.7 convolution_convert_fusion
  14.4 29.7 %all_gather.11 = bf16[2,64,1024]{2,1,0:T(8,128)(2,1)S(1)} all-gather(bf16[2,64,128]{2,1,0:T(8,128)(2,1)S(1)} %bitcast.147), channel_id=1, replica_groups=mesh['group'=2,'tensor'=8,'replica'=2] {'tensor'}, dimensions={2}, use_global_device_ids=true | all-gather | bytes 294912 | tf_op jit(solution)/shard_map/all_gather | solution.py:198
  44.2 0.2 reshape.347
  44.4 0.0 copy-done.5
  44.4 0.1 compare_reduce_fusion
  44.5 0.1 constant_dynamic-slice_fusion.1
  44.6 96.3 %all-gather.3.cloned.1.call-done = bf16[2,16,256,512]{3,2,1,0:T(8,128)(2,1)} async-done(((bf16[2,2,256,512]{3,2,1,0:T(8,128)(2,1)}), bf16[2,16,256,512]{3,2,1,0:T(8,128)(2,1)}) %all-gather.3.cloned.1.call-update) | async-done | bytes 8388624 | tf_op jit(solution)/shard_map/all_gather | solution.py:213
  140.9 3.2 %constant_dynamic-slice_fusion = bf16[2,16,256,128]{3,2,1,0:T(8,128)(2,1)} fusion(bf16[2,16,256,512]{3,2,1,0:T(8,128)(2,1)} %all-gather.3.cloned.1.call-done, s32[]{:T(128)S(6)} %select_n.132), kind=kLoop, calls=%fused_computation.116 | loop fusion | bytes 4194308 | tf_op jit(solution)/shard_map/dynamic_slice | solution.py:214
  144.1 0.0 all-gather.5.cloned.1.call-update
  144.1 0.0 copy-start.6
  144.1 0.0 copy-start.4
  144.2 0.0 copy-start.3
  144.2 12.4 %copy.61 = bf16[512,8192]{1,0:T(8,128)(2,1)} copy(bf16[512,8192]{0,1:T(8,128)(2,1)} %bitcast.135) | data formatting | bytes 16777216 | tf_op jit(solution)/shard_map/dot_general | solution.py:193
  156.6 0.0 copy-done.6
  156.6 0.1 fusion.53
  156.8 0.0 copy-done.4
  156.8 0.3 subtract_convert_fusion.1
  157.1 0.1 maximum_bitcast_fusion
  157.2 0.0 copy-done.3
  157.2 6.3 %fusion.12 = f32[2,64,4,128]{3,1,2,0:T(8,128)S(1)} fusion(bf16[4,128,8192,1]{2,1,0,3:T(8,128)(2,1)} %bitcast.131, bf16[2,64,8192]{2,1,0:T(8,128)(2,1)S(1)} %copy-done.3), kind=kOutput, calls=%fused_computation.18 | convolution fusion | flops 1073741824 | bytes 10747904 | tf_op jit(solution)/shard_map/dot_general | solution.py:193
  163.5 0.2 subtract_convert_fusion
  163.7 0.1 pad_maximum_fusion
  163.8 0.1 fusion.48
  163.9 0.1 fusion.41
  164.0 1.3 fusion.62
  165.4 5.2 %fusion.63 = (f32[2,64,4]{2,0,1:T(2,128)S(1)}, f32[2,64,4,384]{3,2,0,1:T(4,128)S(1)}) fusion(bf16[2,64,384,128]{3,2,1,0:T(8,128)(2,1)} %param.15, bf16[2,64,4,128]{3,1,2,0:T(8,128)(2,1)S(1)} %pad_maximum_fusion, pred[64,384]{1,0:T(8,128)(4,1)S(1)} %fusion.41), kind=kOutput, calls=%fused_computation.122 | convolution fusion | flops 50920960 | bytes 7235584 | tf_op jit(solution)/shard_map/jshd,scd->jshc/dot_general | solution.py:131
  170.6 0.0 all-gather.5.cloned.1.call-done
  170.6 7.5 %gather_fusion = bf16[64,2,256,128]{3,2,1,0:T(8,128)(2,1)} fusion(bf16[2,32,256,128]{3,2,1,0:T(8,128)(2,1)} %all-gather.5.cloned.1.call-done, s32[1024]{0:T(1024)S(1)} %pad_clamp_fusion), kind=kCustom, calls=%fused_computation | custom fusion | bytes 16777472 | tf_op jit(solution)/shard_map/jit(_take)/gather | solution.py:221
  178.1 7.5 %fusion = bf16[2,64,256,128]{3,2,1,0:T(8,128)(2,1)} fusion(bf16[64,2,256,128]{3,2,1,0:T(8,128)(2,1)} %gather_fusion, pred[64]{0:T(512)(128)(4,1)S(1)} %compare_and_fusion), kind=kLoop, calls=%fused_computation.2 | loop fusion | flops 4194304 | bytes 16777280 | tf_op jit(solution)/shard_map/jit(_take)/select_n | solution.py:221
  185.7 0.0 slice-start.2
  185.7 3.7 %fusion.64 = (f32[2,64,4]{2,0,1:T(2,128)S(1)}, f32[2,64,4,256]{3,2,0,1:T(4,128)S(1)}) fusion(bf16[2,64,4,128]{3,1,2,0:T(8,128)(2,1)S(1)} %pad_maximum_fusion, bf16[2,64,256,128]{3,2,1,0:T(8,128)(2,1)} %fusion, pred[64,256]{1,0:T(8,128)(4,1)S(1)} %fusion.48), kind=kOutput, calls=%fused_computation.123 | convolution fusion | flops 33947136 | bytes 4868096 | tf_op jit(solution)/shard_map/jshd,spd->jshp/dot_general | solution.py:135
  189.3 0.3 fusion.42
  189.6 0.6 fusion.35
  190.2 0.4 fusion.36
  190.6 0.0 slice-start.3
  190.6 0.0 slice-start
  190.7 4.3 %fusion.18 = f32[2,64,4,128]{3,2,0,1:T(4,128)S(1)} fusion(bf16[2,64,384,128]{3,2,1,0:T(8,128)(2,1)} %param.15, f32[2,64,4,384]{3,2,0,1:T(4,128)S(1)} %get-tuple-element.20, f32[2,64,4]{2,0,1:T(2,128)S(1)} %bitcast.150, f32[2,64,4]{2,0,1:T(2,128)S(1)} %bitcast.139), kind=kOutput, calls=%fused_computation.22 | convolution fusion | flops 50921472 | bytes 7344128 | tf_op jit(solution)/shard_map/jshc,scd->jshd/dot_general | solution.py:155
  194.9 0.0 slice-done.2
  195.0 0.0 slice-done.3
  195.0 0.0 slice-start.1
  195.0 0.8 fusion.23
  195.8 0.4 fusion.24
  196.2 0.0 copy-start.1
  196.2 0.0 slice-done
  196.3 1.1 slice-done.1
  197.4 31.3 %shard_map.100 = bf16[128,1024]{1,0:T(8,128)(2,1)S(1)} custom-call(bf16[128,512]{1,0:T(8,128)(2,1)S(1)} %bitcast.130, bf16[512,8192]{1,0:T(8,128)(2,1)S(1)} %bitcast.128), custom_call_target="tpu_custom_call" | custom-call | tf_op jit(solution)/shard_map/pallas_call | solution.py:84
  228.7 0.7 copy.93
  229.4 0.0 copy-done.1
  (18 shorter events, 0.2 us)
Async XLA Ops:
  6.5 7.2 %copy-start = (bf16[8192,128]{1,0:T(8,128)(2,1)S(1)}, bf16[8192,128]{1,0:T(8,128)(2,1)}, u32[]{:S(2)}) copy-start(bf16[8192,128]{1,0:T(8,128)(2,1)} %param.13) | copy-start | bytes 6291460
  6.5 134.4 %all-gather.3.cloned.1.call-start = ((), (), s32[]{:S(2)}) async-start(), calls=%async_computation | async-start | bytes 9437184 | tf_op jit(solution)/shard_map/all_gather | solution.py:213
  7.3 163.3 %all-gather.5.cloned.1.call-start = ((), (), s32[]{:S(2)}) async-start(), calls=%async_computation.1 | async-start | bytes 6291456 | tf_op jit(solution)/shard_map/all_gather | solution.py:215
  10.2 34.2 %copy-start.5 = (s32[32]{0:T(128)S(1)}, s32[32]{0:T(128)}, u32[]{:S(2)}) copy-start(s32[32]{0:T(128)} %param.19) | copy-start | bytes 388
  12.4 1.3 copy-start.2
  144.1 12.5 %copy-start.6 = (s32[32]{0:T(128)S(1)}, s32[32]{0:T(128)}, u32[]{:S(2)}) copy-start(s32[32]{0:T(128)} %param.18) | copy-start | bytes 388
  144.1 12.6 %copy-start.4 = (s32[64]{0:T(128)S(1)}, s32[64]{0:T(128)}, u32[]{:S(2)}) copy-start(s32[64]{0:T(128)} %param.16) | copy-start | bytes 772
  144.2 13.1 %copy-start.3 = (bf16[2,64,8192]{2,1,0:T(8,128)(2,1)S(1)}, bf16[2,64,8192]{2,1,0:T(8,128)(2,1)}, u32[]{:S(2)}) copy-start(bf16[2,64,8192]{2,1,0:T(8,128)(2,1)} %copy-done.2) | copy-start | bytes 6291460
  185.7 9.3 %slice-start.2 = ((s8[8388608]{0:T(1024)(128)(4,1)}), s8[4194304]{0:T(1024)(128)(4,1)S(1)}, s32[]{:S(2)}) async-start(s8[8388608]{0:T(1024)(128)(4,1)} %bitcast.133), calls=%async_computation.4 | async-start | bytes 8388608
  190.6 4.3 %slice-start.3 = ((s8[8388608]{0:T(1024)(128)(4,1)}), s8[4194304]{0:T(1024)(128)(4,1)S(1)}, s32[]{:S(2)}) async-start(s8[8388608]{0:T(1024)(128)(4,1)} %bitcast.133), calls=%async_computation.5 | async-start | bytes 8388608
  190.6 5.6 %slice-start = ((s8[8388608]{0:T(1024)(128)(4,1)}), s8[4194304]{0:T(1024)(128)(4,1)S(1)}, s32[]{:S(2)}) async-start(s8[8388608]{0:T(1024)(128)(4,1)} %bitcast.127), calls=%async_computation.2 | async-start | bytes 8388608
  195.0 2.4 %slice-start.1 = ((s8[8388608]{0:T(1024)(128)(4,1)}), s8[4194304]{0:T(1024)(128)(4,1)S(1)}, s32[]{:S(2)}) async-start(s8[8388608]{0:T(1024)(128)(4,1)} %bitcast.127), calls=%async_computation.3 | async-start | bytes 8388608
  196.2 33.1 %copy-start.1 = (bf16[8192,128]{1,0:T(8,128)(2,1)S(1)}, bf16[8192,128]{1,0:T(8,128)(2,1)}, u32[]{:S(2)}) copy-start(bf16[8192,128]{1,0:T(8,128)(2,1)} %param.13) | copy-start | bytes 6291460
Sparse Core Ops, SparseCore 0:
  9.5 131.3 all-gather.2
  144.2 11.8 all-gather.4

commit v2 on v1

--- a/solution.py
+++ b/solution.py
@@ -102,67 +102,238 @@
         compiler_params=pltpu.CompilerParams(collective_id=1, has_side_effects=True, vmem_limit_bytes=40 * 2**20),
     )(heads, w_out)
 
-
-def rotate(values, positions):
-    half_dim = values.shape[-1] // 2
-    freqs = THETA ** (-2.0 * jnp.arange(half_dim, dtype=jnp.float32) / values.shape[-1])
-    angles = positions[..., None].astype(jnp.float32) * freqs
-    cosine = jnp.cos(angles)
-    sine = jnp.sin(angles)
-    first = values[..., :half_dim]
-    second = values[..., half_dim:]
-    return jnp.concatenate([first * cosine - second * sine, second * cosine + first * sine], -1)
-
-
-def attend(
-    queries,
-    cache_keys,
-    cache_values,
-    prompt_keys,
-    prompt_values,
-    new_keys,
-    new_values,
-    cache_valid,
-    prompt_valid,
-    own_valid,
+def attend(query, keys, values, length, own_keys, own_values, local_heads):
+    scaling = HD ** (-0.5)
+    score = lax.dot_general(
+        query.astype(jnp.bfloat16), keys, (((1,), (1,)), ((), ())), preferred_element_type=jnp.float32
+    ) * scaling
+    score = jnp.where(lax.broadcasted_iota(jnp.int32, score.shape, 1) < length, score, NEGATIVE)
+    step_of = lax.broadcasted_iota(jnp.int32, (query.shape[0], 1), 0) // local_heads
+    own = []
+    for step, key in enumerate(own_keys):
+        one = jnp.sum(query * key, axis=1, keepdims=True) * scaling
+        own.append(jnp.where(step_of >= step, one, NEGATIVE))
+    top = jnp.max(score, axis=1, keepdims=True)
+    for one in own:
+        top = jnp.maximum(top, one)
+    score = jnp.exp(score - top)
+    own = [jnp.exp(one - top) for one in own]
+    summed = jnp.sum(score, axis=1, keepdims=True)
+    for one in own:
+        summed = summed + one
+    inverse = 1.0 / summed
+    result = jnp.dot((score * inverse).astype(jnp.bfloat16), values, preferred_element_type=jnp.float32)
+    for one, value in zip(own, own_values):
+        result = result + (one * inverse).astype(jnp.bfloat16).astype(jnp.float32) * value
+    return result
+
+
+def attend_kernel(
+    size, length_ref, plength_ref, local_ref, request_ref, matched_ref,
+    query_ref, part_ref, cosine_ref, sine_ref, cache_ref, prompt_ref, heads_ref,
+    cache, prompts, parts, new_keys, new_values, cache_out, prompt_out,
+    csem, lsem, p1s, p1r, p2s, p2r, p3s, p3r, ks, kr,
 ):
-    scaling = HD ** (-0.5)
-    score_cache = (
-        jnp.einsum("jshd,scd->jshc", queries, cache_keys, preferred_element_type=jnp.float32)
-        * scaling
-    )
-    score_prompt = (
-        jnp.einsum("jshd,spd->jshp", queries, prompt_keys, preferred_element_type=jnp.float32)
-        * scaling
-    )
-    score_own = (
-        jnp.einsum("jshd,isd->jshi", queries, new_keys, preferred_element_type=jnp.float32)
-        * scaling
-    )
-    score_cache = jnp.where(cache_valid[None, :, None, :], score_cache, NEGATIVE)
-    score_prompt = jnp.where(prompt_valid[None, :, None, :], score_prompt, NEGATIVE)
-    score_own = jnp.where(own_valid[:, None, None, :], score_own, NEGATIVE)
-    top = jnp.maximum(
-        jnp.maximum(jnp.max(score_cache, -1), jnp.max(score_prompt, -1)), jnp.max(score_own, -1)
-    )[..., None]
-    exp_cache = jnp.exp(score_cache - top)
-    exp_prompt = jnp.exp(score_prompt - top)
-    exp_own = jnp.exp(score_own - top)
-    summed = (jnp.sum(exp_cache, -1) + jnp.sum(exp_prompt, -1) + jnp.sum(exp_own, -1))[..., None]
-    weight_cache = (exp_cache / summed).astype(jnp.bfloat16)
-    weight_prompt = (exp_prompt / summed).astype(jnp.bfloat16)
-    weight_own = (exp_own / summed).astype(jnp.bfloat16)
-    result = jnp.einsum(
-        "jshc,scd->jshd", weight_cache, cache_values, preferred_element_type=jnp.float32
-    )
-    result = result + jnp.einsum(
-        "jshp,spd->jshd", weight_prompt, prompt_values, preferred_element_type=jnp.float32
-    )
-    result = result + jnp.einsum(
-        "jshi,isd->jshd", weight_own, new_values, preferred_element_type=jnp.float32
-    )
-    return result.astype(jnp.bfloat16)
-
+    slots, head_rows, _ = query_ref.shape
+    steps = new_keys.shape[0]
+    local_heads = head_rows // steps
+    kv_heads = prompt_ref.shape[3] // HD
+    per_device = prompt_ref.shape[1]
+    share = size // kv_heads
+    pieces = parts.shape[1]
+    rank = lax.axis_index("tensor")
+    copy_of = lax.axis_index("replica")
+    head = rank // share
+    side = lax.rem(rank, share)
+    offsets = [0] + list(range(kv_heads // 2, kv_heads)) + list(range(1, kv_heads // 2))
+    chunk = 8
+
+    loads = []
+    chunks = slots // chunk
+    for at in range(chunks):
+        rows = pl.ds(at * chunk, chunk)
+        copy = pltpu.make_async_copy(cache_ref.at[:, rows], cache.at[:, rows], csem.at[at])
+        copy.start()
+        loads.append(copy)
+
+    barrier = pltpu.get_barrier_semaphore()
+    for off in range(1, size):
+        pl.semaphore_signal(barrier, inc=1, device_id={"tensor": lax.rem(rank + off, size)}, device_id_type=MESH)
+    pl.semaphore_signal(barrier, inc=1, device_id={"replica": 1 - copy_of}, device_id_type=MESH)
+    pl.semaphore_wait(barrier, size)
+
+    column = rank // pieces
+    kind = column // kv_heads
+    piece = lax.rem(rank, pieces)
+    part_copies = []
+    for at in range(share):
+        target = lax.rem(column, kv_heads) * share + at
+        remote = pltpu.make_async_remote_copy(
+            src_ref=part_ref, dst_ref=parts.at[kind, piece], send_sem=ks.at[at], recv_sem=kr.at[kind, piece],
+            device_id={"tensor": target}, device_id_type=MESH)
+        part_copies.append((target, remote))
+
+        @pl.when(target != rank)
+        def _(remote=remote):
+            remote.start()
+
+        @pl.when(target == rank)
+        def _():
+            pltpu.make_async_copy(part_ref, parts.at[kind, piece], kr.at[kind, piece]).start()
+
+    def slot_of(plane, side_at, replica_at):
+        return (plane * share + side_at) * 2 + replica_at
+
+    def arrive(slot, sem):
+        pltpu.make_async_copy(prompts.at[slot], prompts.at[slot], sem).wait()
+
+    sent = []
+
+    def send(src, slot, send_sem, recv_sem, device):
+        copy = pltpu.make_async_remote_copy(
+            src_ref=src, dst_ref=prompts.at[slot], send_sem=send_sem, recv_sem=recv_sem,
+            device_id=device, device_id_type=MESH)
+        copy.start()
+        sent.append(copy)
+
+    def plane_of(at):
+        return lax.rem(head + kv_heads - offsets[at], kv_heads)
+
+    def slab(which):
+        return prompt_ref.at[:, :, :, pl.ds(pl.multiple_of(which * HD, HD), HD)]
+
+    mine = slot_of(head, side, copy_of)
+    for at in range(1, kv_heads):
+        target = lax.rem(head + offsets[at], kv_heads)
+        send(slab(target), mine, p1s.at[at], p1r.at[at], {"tensor": target * share + side})
+    keep = pltpu.make_async_copy(slab(head), prompts.at[mine], lsem)
+    keep.start()
+
+    def spread(at, src, slot):
+        for other in range(1, share):
+            target = head * share + lax.rem(side + other, share)
+            send(src, slot, p2s.at[other, at], p2r.at[other, at], {"tensor": target})
+        send(src, slot, p3s.at[0, at], p3r.at[0, at], {"replica": 1 - copy_of})
+
+    def pass_on(at):
+        for other in range(1, share):
+            slot = slot_of(plane_of(at), lax.rem(side + share - other, share), copy_of)
+            arrive(slot, p2r.at[other, at])
+            send(prompts.at[slot], slot, p3s.at[other, at], p3r.at[other, at], {"replica": 1 - copy_of})
+
+    spread(0, slab(head), mine)
+
+    for which in range(2):
+        for at in range(pieces):
+            pltpu.make_async_copy(parts.at[which, at], parts.at[which, at], kr.at[which, at]).wait()
+    joined = [
+        jnp.concatenate([parts[which, at] for at in range(pieces)], axis=1).astype(jnp.float32)
+        for which in range(2)
+    ]
+    turned = joined[0] * cosine_ref[...] + pltpu.roll(joined[0], HD // 2, 1) * sine_ref[...]
+    turned = turned.astype(jnp.bfloat16).astype(jnp.float32)
+    for step in range(steps):
+        new_keys[step] = turned[step * slots:(step + 1) * slots]
+        new_values[step] = joined[1][step * slots:(step + 1) * slots]
+
+    def own_of(slot):
+        row = pl.ds(slot, 1)
+        return [new_keys[i, row, :] for i in range(steps)], [new_values[i, row, :] for i in range(steps)]
+
+    def cache_chunk(at, carry):
+        for inner in range(chunk):
+            slot = at * chunk + inner
+            keys, values = own_of(slot)
+            cache_out[slot] = attend(
+                query_ref[slot], cache[0, slot], cache[1, slot], length_ref[slot], keys, values, local_heads)
+        return carry
+
+    groups = kv_heads
+    each = chunks // groups
+    for group in range(groups):
+        if group + 1 < kv_heads:
+            slot = slot_of(plane_of(group + 1), side, copy_of)
+            arrive(slot, p1r.at[group + 1])
+            spread(group + 1, prompts.at[slot], slot)
+        pass_on(group)
+        for at in range(group * each, (group + 1) * each):
+            loads[at].wait()
+        lax.fori_loop(group * each, (group + 1) * each, cache_chunk, 0)
+
+    keep.wait()
+    per_plane = share * 2 * per_device
+    batch = min(8, per_plane)
+    for group in range(kv_heads):
+        plane = plane_of(group)
+        for other in range(share):
+            arrive(slot_of(plane, lax.rem(side + share - other, share), 1 - copy_of), p3r.at[other, group])
+
+        def prompt_chunk(at, carry, plane=plane):
+            for inner in range(batch):
+                sender = plane * (share * 2) + at * (batch // per_device) + inner // per_device
+                within = inner % per_device
+                request = sender * per_device + within
+                slot = local_ref[request]
+                keys, values = own_of(slot)
+                prompt_out[request] = attend(
+                    query_ref[slot], prompts[sender, 0, within], prompts[sender, 1, within],
+                    plength_ref[request], keys, values, local_heads)
+            return carry
+
+        lax.fori_loop(0, per_plane // batch, prompt_chunk, 0)
+
+    def choose(slot, carry):
+        cache_out[slot] = jnp.where(matched_ref[slot] > 0, prompt_out[request_ref[slot]], cache_out[slot])
+        return carry
+
+    lax.fori_loop(0, slots, choose, 0)
+    for step in range(steps):
+        for at in range(local_heads):
+            heads_ref[pl.ds(step * slots, slots), pl.ds(at * HD, HD)] = cache_out[
+                :, step * local_heads + at, :].astype(jnp.bfloat16)
+
+    for copy in sent:
+        copy.wait_send()
+    for target, copy in part_copies:
+        @pl.when(target != rank)
+        def _(copy=copy):
+            copy.wait_send()
+
+
+def attention(lengths, plengths, local_slot, request, matched, queries, part, cosine, sine, cache_kv, prompt_kv, size):
+    slots, head_rows, _ = queries.shape
+    rows, width = part.shape
+    steps = rows // slots
+    kv_heads = prompt_kv.shape[3] // HD
+    share = size // kv_heads
+    requests = plengths.shape[0]
+    senders = requests // prompt_kv.shape[1]
+    smem = pl.BlockSpec(memory_space=pltpu.SMEM)
+    vmem = pl.BlockSpec(memory_space=pltpu.VMEM)
+    hbm = pl.BlockSpec(memory_space=pl.ANY)
+    dma = pltpu.SemaphoreType.DMA
+    return pl.pallas_call(
+        functools.partial(attend_kernel, size),
+        out_shape=jax.ShapeDtypeStruct((rows, head_rows // steps * HD), jnp.bfloat16),
+        in_specs=[smem] * 5 + [vmem] * 4 + [hbm] * 2,
+        out_specs=vmem,
+        scratch_shapes=[
+            pltpu.VMEM(cache_kv.shape, jnp.bfloat16),
+            pltpu.VMEM((senders, 2, prompt_kv.shape[1], prompt_kv.shape[2], HD), jnp.bfloat16),
+            pltpu.VMEM((2, HD // width, rows, width), jnp.bfloat16),
+            pltpu.VMEM((steps, slots, HD), jnp.float32),
+            pltpu.VMEM((steps, slots, HD), jnp.float32),
+            pltpu.VMEM(queries.shape, jnp.float32),
+            pltpu.VMEM((requests, head_rows, HD), jnp.float32),
+            dma((slots // 8,)),
+            dma,
+            dma((kv_heads,)), dma((kv_heads,)),
+            dma((share, kv_heads)), dma((share, kv_heads)),
+            dma((share, kv_heads)), dma((share, kv_heads)),
+            dma((share,)), dma((2, HD // width)),
+        ],
+        compiler_params=pltpu.CompilerParams(collective_id=2, has_side_effects=True, vmem_limit_bytes=48 * 2**20),
+    )(lengths, plengths, local_slot, request, matched, queries, part, cosine, sine, cache_kv, prompt_kv)
 
 def local(
     hidden_in,
@@ -177,15 +348,9 @@
     slot_of,
 ):
     tensor_size = lax.axis_size("tensor")
-    replica_size = lax.axis_size("replica")
-    tensor_rank = lax.axis_index("tensor")
     replica_rank = lax.axis_index("replica")
     step_count, row_count, model_width = hidden_in.shape
     local_heads = w_query.shape[1] // HD
-    kv_head = tensor_rank * local_heads // GROUP
-    per_device = prompt_kv.shape[1]
-    prompt_cap = prompt_kv.shape[2]
-    capacity = cache_kv.shape[2]
     hidden = hidden_in.astype(jnp.float32)
     scale = lax.rsqrt(jnp.mean(hidden * hidden, -1, keepdims=True) + EPSILON)
     normed = (hidden * scale * norm_gain.astype(jnp.float32)).astype(jnp.bfloat16)
@@ -194,11 +359,6 @@
         step_count, row_count, local_heads, HD
     )
     keyval_part = jnp.dot(flat, w_keyval, preferred_element_type=jnp.float32).astype(jnp.bfloat16)
-    keyval_part = keyval_part.reshape(step_count, row_count, -1)
-    keyval = lax.all_gather(keyval_part, "tensor", axis=2, tiled=True).reshape(
-        step_count, row_count, 2, KVH, HD
-    )
-    own_pair = lax.dynamic_index_in_dim(keyval, kv_head, 3, keepdims=False)
     slot_ids = replica_rank * row_count + jnp.arange(row_count, dtype=jnp.int32)
     matches = slot_of[None, :] == slot_ids[:, None]
     matched = jnp.any(matches, 1)
@@ -207,41 +367,32 @@
     prompt_len = jnp.sum(jnp.where(matches, block_count[None, :], 0), 1) * BLOCK
     base_pos = jnp.where(matched, prompt_len, cache_len)
     positions = base_pos[None, :] + jnp.arange(step_count, dtype=jnp.int32)[:, None]
-    queries = rotate(queries, positions[:, :, None]).astype(jnp.bfloat16)
-    new_keys = rotate(own_pair[:, :, 0].astype(jnp.float32), positions).astype(jnp.bfloat16)
-    new_values = own_pair[:, :, 1]
-    everything = lax.all_gather(prompt_kv, "tensor", axis=1, tiled=True)
-    own_prompts = lax.dynamic_slice_in_dim(everything, kv_head * HD, HD, 3)
-    paired = lax.all_gather(own_prompts, "replica", axis=1, tiled=True)
-    sender = request // per_device
-    within = request % per_device
-    sender_tensor = sender // replica_size
-    sender_replica = sender % replica_size
-    position = (sender_replica * tensor_size + sender_tensor) * per_device + within
-    chosen = jnp.take(paired, position, axis=1)
-    cache_valid = jnp.logical_not(matched)[:, None] & (
-        jnp.arange(capacity, dtype=jnp.int32)[None, :] < cache_len[:, None]
+    half_dim = HD // 2
+    freqs = THETA ** (-2.0 * jnp.arange(half_dim, dtype=jnp.float32) / HD)
+    angles = positions[..., None].astype(jnp.float32) * freqs
+    cosine = jnp.cos(angles)
+    sine = jnp.sin(angles)
+    cosine = jnp.concatenate([cosine, cosine], -1)
+    sine = jnp.concatenate([-sine, sine], -1)
+    swapped = jnp.concatenate([queries[..., half_dim:], queries[..., :half_dim]], -1)
+    queries = queries * cosine[:, :, None] + swapped * sine[:, :, None]
+    queries = queries.astype(jnp.bfloat16).astype(jnp.float32)
+    queries = queries.transpose(1, 0, 2, 3).reshape(row_count, step_count * local_heads, HD)
+    local_slot = jnp.clip(slot_of - replica_rank * row_count, 0, row_count - 1)
+    heads_flat = attention(
+        cache_len,
+        block_count * BLOCK,
+        local_slot,
+        request,
+        matched.astype(jnp.int32),
+        queries,
+        keyval_part,
+        cosine.reshape(step_count * row_count, HD),
+        sine.reshape(step_count * row_count, HD),
+        cache_kv,
+        prompt_kv,
+        tensor_size,
     )
-    prompt_valid = matched[:, None] & (
-        jnp.arange(prompt_cap, dtype=jnp.int32)[None, :] < prompt_len[:, None]
-    )
-    own_valid = (
-        jnp.arange(step_count, dtype=jnp.int32)[None, :]
-        <= jnp.arange(step_count, dtype=jnp.int32)[:, None]
-    )
-    heads_out = attend(
-        queries,
-        cache_kv[0],
-        cache_kv[1],
-        chosen[0],
-        chosen[1],
-        new_keys,
-        new_values,
-        cache_valid,
-        prompt_valid,
-        own_valid,
-    )
-    heads_flat = heads_out.reshape(step_count * row_count, local_heads * HD)
     mixed = project_out(heads_flat, w_out, tensor_size)
     return mixed.reshape(step_count, row_count, -1)
 

time: 237 us -> 122 us (0.51)
  waiting for transfers between devices: 97 us -> 0 us
  Pallas kernels: 31.3 us -> 91.7 us
  blocking collectives: 29.7 us -> 0 us
  matrix products: 22.6 us -> 7.16 us
  between operations: 13.8 us -> 0.18 us
  local copies, waits for them, and re-layouts: 26.7 us -> 16.1 us
  other arithmetic: 15 us -> 6.18 us
    all_gather x2 -> x0, waiting for transfers between devices: 96.3 us -> none  [the longest x1 96.3 us: local(): everything = lax.all_gather(prompt_kv, 'tensor', axis=1, tiled=True)]
    pallas_call x0 -> x1, Pallas kernels: none -> 61.3 us  [attention(): pl.pallas_call(functools.partial(attend_kernel, size), out_shape=jax.Shap...]
    all_gather x1 -> x0, blocking collectives: 29.7 us -> none  [local(): lax.all_gather(keyval_part, 'tensor', axis=2, tiled=True)]
    dot_general x6 -> x0, matrix products: 15.6 us -> none  [the longest x1 5.18 us: attend(): jnp.einsum('jshd,scd->jshc', queries, cache_keys, preferred_element_type=...]
    select_n x2 -> x1, other arithmetic: 7.57 us -> 0.01 us  [local(): base_pos = jnp.where(matched, prompt_len, cache_len)]
    gather x1 -> x0, local copies, waits for them, and re-layouts: 7.53 us -> none  [local(): chosen = jnp.take(paired, position, axis=1)]
    dynamic_slice x3 -> x0, local copies, waits for them, and re-layouts: 3.33 us -> none  [the longest x1 3.18 us: local(): own_prompts = lax.dynamic_slice_in_dim(everything, kv_head * HD, HD, 3)]
  transfers between devices with their start and end apart: 2 -> 0, of which waited for: 1 -> 0; matrix products, arithmetic and copies ran while one was open for 14% -> 0% of each run, Pallas kernels for 0% -> 0%
where the time goes in v2:
time: 122 us; the launch traced here: 121 us
  Pallas kernels  91.7 us (75%)
  local copies, waits for them, and re-layouts  16.1 us (13%)
  matrix products  7.16 us (6%)
  other arithmetic  6.18 us (5%)
    pallas_call x1, Pallas kernels, attention(): pl.pallas_call(functools.partial(attend_kernel, size), out_shape=jax.Shap...  61.3 us
    pallas_call x1, Pallas kernels, project_out(): pl.pallas_call(functools.partial(out_kernel, size), out_shape=jax.ShapeDt...  30.3 us
    dot_general x1, local copies, waits for them, and re-layouts, local(): jnp.dot(flat, w_query, preferred_element_type=jnp.float32)  11.6 us
    dot_general x1, matrix products, local(): jnp.dot(flat, w_query, preferred_element_type=jnp.float32)  6.42 us
    unnamed x13, local copies, waits for them, and re-layouts  4.11 us

profile of v2, /device:TPU:0, one launch (start us, length us, event | category | flops | bytes accessed | tf_op | source)
XLA Modules:
  0.0 121.3 jit_solution(18195873802919163935)
XLA Ops:
  0.0 0.0 copy-start
  0.0 0.8 subtract_clamp_fusion
  0.8 0.8 fusion.10
  1.6 0.7 compare_reduce_fusion
  2.3 0.0 copy-start.5
  2.4 11.6 %copy.16 = bf16[512,8192]{1,0:T(8,128)(2,1)} copy(bf16[512,8192]{0,1:T(8,128)(2,1)} %bitcast.23) | data formatting | bytes 16777216 | tf_op jit(solution)/shard_map/dot_general | solution.py:358
  13.9 0.0 copy-start.4
  13.9 0.0 copy-done.5
  13.9 2.3 %fusion = f32[2,64]{1,0:T(2,128)S(1)} fusion(bf16[2,64,8192]{2,1,0:T(8,128)(2,1)} %param.10), kind=kLoop, calls=%fused_computation.2 | loop fusion | flops 3145600 | bytes 2097664 | tf_op jit(solution)/shard_map/reduce_sum | solution.py:355
  16.2 0.0 copy-done.4
  16.2 0.6 fusion.2
  16.8 0.0 copy-start.3
  16.8 6.4 %fusion.3 = f32[2,64,4,128]{3,1,2,0:T(8,128)S(1)} fusion(bf16[4,128,8192,1]{2,1,0,3:T(8,128)(2,1)} %bitcast.21, bf16[2,64,8192]{2,1,0:T(8,128)(2,1)S(1)} %fusion.2), kind=kOutput, calls=%fused_computation.5 | convolution fusion | flops 1073741824 | bytes 10747904 | tf_op jit(solution)/shard_map/dot_general | solution.py:358
  23.2 0.1 fusion.11
  23.4 0.0 copy-done.3
  23.4 0.3 multiply_cosine_fusion.1
  23.7 0.1 pad_maximum_fusion
  23.8 0.1 convert_bitcast_fusion
  24.0 0.2 copy.14
  24.2 0.0 copy-done
  24.2 0.0 copy-start.2
  24.2 0.7 convolution_convert_fusion.part_ref
  24.9 0.1 add.61
  25.0 0.1 add.63
  25.1 0.3 fusion.7
  25.4 0.1 pad_maximum_fusion.2
  25.6 0.0 copy-done.2
  25.6 61.3 %shard_map.100.heads_ref = bf16[128,512]{1,0:T(8,128)(2,1)S(1)} custom-call(s32[64]{0:T(128)S(1)} %copy-done.3, s32[32]{0:T(128)S(1)} %get-tuple-element.20.plength_ref, s32[32]{0:T(128)S(1)} %get-tuple-element.19.local_ref, s32[64]{0:T(128)S(1)} %get-tuple-element.6.request_ref, s32[64]{0:T(128)S(1)} %convert_element_type.30.matched_ref, ...), custom_call_target="tpu_custom_call" | custom-call | tf_op jit(solution)/shard_map/pallas_call | solution.py:315
  86.9 0.0 copy-start.1
  86.9 3.4 %copy-done.1 = bf16[512,8192]{1,0:T(8,128)(2,1)S(1)} copy-done((bf16[512,8192]{1,0:T(8,128)(2,1)S(1)}, bf16[512,8192]{1,0:T(8,128)(2,1)}, u32[]{:S(2)}) %copy-start.1) | copy-done | bytes 8388632
  90.3 30.3 %shard_map.101 = bf16[128,1024]{1,0:T(8,128)(2,1)S(1)} custom-call(bf16[128,512]{1,0:T(8,128)(2,1)S(1)} %shard_map.100.heads_ref, bf16[512,8192]{1,0:T(8,128)(2,1)S(1)} %copy-done.1), custom_call_target="tpu_custom_call" | custom-call | tf_op jit(solution)/shard_map/pallas_call | solution.py:84
  120.6 0.7 copy.18
  (10 shorter events, 0.1 us)
Async XLA Ops:
  0.0 24.2 %copy-start = (bf16[8192,128]{1,0:T(8,128)(2,1)S(1)}, bf16[8192,128]{1,0:T(8,128)(2,1)}, u32[]{:S(2)}) copy-start(bf16[8192,128]{1,0:T(8,128)(2,1)} %param.13) | copy-start | bytes 6291460
  2.3 11.6 %copy-start.5 = (bf16[8192]{0:T(1024)(128)(2,1)S(1)}, bf16[8192]{0:T(1024)(128)(2,1)}, u32[]{:S(2)}) copy-start(bf16[8192]{0:T(1024)(128)(2,1)} %param.11) | copy-start | bytes 49156
  13.9 2.3 %copy-start.4 = (bf16[2,64,8192]{2,1,0:T(8,128)(2,1)S(1)}, bf16[2,64,8192]{2,1,0:T(8,128)(2,1)}, u32[]{:S(2)}) copy-start(bf16[2,64,8192]{2,1,0:T(8,128)(2,1)} %param.10) | copy-start | bytes 6291460
  16.8 6.6 %copy-start.3 = (s32[64]{0:T(128)S(1)}, s32[64]{0:T(128)}, u32[]{:S(2)}) copy-start(s32[64]{0:T(128)} %length_ref.1) | copy-start | bytes 772
  24.2 1.4 %copy-start.2 = (bf16[2,2,256,512]{3,2,1,0:T(8,128)(2,1)S(1)}, bf16[2,2,256,512]{3,2,1,0:T(8,128)(2,1)}, u32[]{:S(2)}) copy-start(bf16[2,2,256,512]{3,2,1,0:T(8,128)(2,1)} %prompt_ref.1) | copy-start | bytes 3145732
  86.9 3.4 %copy-start.1 = (bf16[512,8192]{1,0:T(8,128)(2,1)S(1)}, bf16[512,8192]{1,0:T(8,128)(2,1)}, u32[]{:S(2)}) copy-start(bf16[512,8192]{1,0:T(8,128)(2,1)} %w_ref.1) | copy-start | bytes 25165828

commit v3 on v2

--- a/solution.py
+++ b/solution.py
@@ -19,13 +19,11 @@
 MESH = pl.DeviceIdType.MESH
 
 
-def out_kernel(size, heads_ref, w_ref, out_ref, wbuf, own, send1, recv1, send2, recv2, wsem, s1s, s1r, s2s, s2r):
+def load_out(size, w_ref, wbuf, wsem, width):
     half = size // 2
     rank = lax.axis_index("tensor")
     mine = rank // 2
     side = lax.rem(rank, 2)
-    partner = rank + 1 - 2 * side
-    width = out_ref.shape[1]
     offsets = [o for o in range(half // 2, half)] + [o for o in range(1, half // 2)] + [0]
 
     weights = []
@@ -36,12 +34,16 @@
             copy = pltpu.make_async_copy(w_ref.at[:, columns], wbuf.at[at, which], wsem.at[at, which])
             copy.start()
             weights.append(copy)
-
-    barrier = pltpu.get_barrier_semaphore()
-    peers = [partner] + [2 * lax.rem(mine + off, half) + side for off in range(1, half)]
-    for peer in peers:
-        pl.semaphore_signal(barrier, inc=1, device_id={"tensor": peer}, device_id_type=MESH)
-    pl.semaphore_wait(barrier, len(peers))
+    return weights
+
+
+def project_out(size, weights, heads_ref, out_ref, wbuf, own, send1, recv1, send2, recv2, s1s, s1r, s2s, s2r):
+    half = size // 2
+    rank = lax.axis_index("tensor")
+    mine = rank // 2
+    side = lax.rem(rank, 2)
+    partner = rank + 1 - 2 * side
+    offsets = [o for o in range(half // 2, half)] + [o for o in range(1, half // 2)] + [0]
 
     heads = heads_ref[...]
     first = []
@@ -77,31 +79,6 @@
         copy.wait_send()
 
 
-def project_out(heads, w_out, size):
-    rows, depth = heads.shape
-    width = w_out.shape[1] // size
-    half = size // 2
-    return pl.pallas_call(
-        functools.partial(out_kernel, size),
-        out_shape=jax.ShapeDtypeStruct((rows, width), jnp.bfloat16),
-        in_specs=[pl.BlockSpec(memory_space=pltpu.VMEM), pl.BlockSpec(memory_space=pl.ANY)],
-        out_specs=pl.BlockSpec(memory_space=pltpu.VMEM),
-        scratch_shapes=[
-            pltpu.VMEM((half, 2, depth, width), jnp.bfloat16),
-            pltpu.VMEM((half, rows, width), jnp.float32),
-            pltpu.VMEM((half, rows, width), jnp.bfloat16),
-            pltpu.VMEM((half, rows, width), jnp.bfloat16),
-            pltpu.VMEM((half - 1, rows, width), jnp.bfloat16),
-            pltpu.VMEM((half - 1, rows, width), jnp.bfloat16),
-            pltpu.SemaphoreType.DMA((half, 2)),
-            pltpu.SemaphoreType.DMA((half,)),
-            pltpu.SemaphoreType.DMA((half,)),
-            pltpu.SemaphoreType.DMA((half - 1,)),
-            pltpu.SemaphoreType.DMA((half - 1,)),
-        ],
-        compiler_params=pltpu.CompilerParams(collective_id=1, has_side_effects=True, vmem_limit_bytes=40 * 2**20),
-    )(heads, w_out)
-
 def attend(query, keys, values, length, own_keys, own_values, local_heads):
     scaling = HD ** (-0.5)
     score = lax.dot_general(
@@ -128,13 +105,16 @@
     return result
 
 
-def attend_kernel(
+def whole_kernel(
     size, length_ref, plength_ref, local_ref, request_ref, matched_ref,
-    query_ref, part_ref, cosine_ref, sine_ref, cache_ref, prompt_ref, heads_ref,
+    gain_ref, cosine_ref, sine_ref, hidden_ref, wq_ref, wkv_ref, cache_ref, prompt_ref, w_ref, out_ref,
+    normed, wq, wkv, query_sum, part_sum, part_ref, query_ref, heads_ref,
     cache, prompts, parts, new_keys, new_values, cache_out, prompt_out,
-    csem, lsem, p1s, p1r, p2s, p2r, p3s, p3r, ks, kr,
+    wbuf, own_sum, send1, recv1, send2, recv2,
+    hsem, qsem, vsem, csem, lsem, p1s, p1r, p2s, p2r, p3s, p3r, ks, kr, wsem, s1s, s1r, s2s, s2r,
 ):
     slots, head_rows, _ = query_ref.shape
+    depth = wq.shape[0] // qsem.shape[0]
     steps = new_keys.shape[0]
     local_heads = head_rows // steps
     kv_heads = prompt_ref.shape[3] // HD
@@ -148,6 +128,71 @@
     offsets = [0] + list(range(kv_heads // 2, kv_heads)) + list(range(1, kv_heads // 2))
     chunk = 8
 
+    hidden_loads = []
+    for step in range(steps):
+        copy = pltpu.make_async_copy(hidden_ref.at[step], normed.at[pl.ds(step * slots, slots)], hsem.at[step])
+        copy.start()
+        hidden_loads.append(copy)
+
+    def weight_loads(at):
+        deep = pl.ds(pl.multiple_of(at * depth, depth), depth)
+        return (
+            pltpu.make_async_copy(wq_ref.at[deep], wq.at[deep], qsem.at[at]),
+            pltpu.make_async_copy(wkv_ref.at[deep], wkv.at[deep], vsem.at[at]),
+        )
+
+    for at in range(qsem.shape[0]):
+        for copy in weight_loads(at):
+            copy.start()
+
+    barrier = pltpu.get_barrier_semaphore()
+    for off in range(1, size):
+        pl.semaphore_signal(barrier, inc=1, device_id={"tensor": lax.rem(rank + off, size)}, device_id_type=MESH)
+    pl.semaphore_signal(barrier, inc=1, device_id={"replica": 1 - copy_of}, device_id_type=MESH)
+    pl.semaphore_wait(barrier, size)
+
+    def slot_of(plane, side_at, replica_at):
+        return (plane * share + side_at) * 2 + replica_at
+
+    def arrive(slot, sem):
+        pltpu.make_async_copy(prompts.at[slot], prompts.at[slot], sem).wait()
+
+    sent = []
+
+    def send(src, slot, send_sem, recv_sem, device):
+        copy = pltpu.make_async_remote_copy(
+            src_ref=src, dst_ref=prompts.at[slot], send_sem=send_sem, recv_sem=recv_sem,
+            device_id=device, device_id_type=MESH)
+        copy.start()
+        sent.append(copy)
+
+    def plane_of(at):
+        return lax.rem(head + kv_heads - offsets[at], kv_heads)
+
+    def slab(which):
+        return prompt_ref.at[:, :, :, pl.ds(pl.multiple_of(which * HD, HD), HD)]
+
+    mine = slot_of(head, side, copy_of)
+    for at in range(1, kv_heads):
+        target = lax.rem(head + offsets[at], kv_heads)
+        send(slab(target), mine, p1s.at[at], p1r.at[at], {"tensor": target * share + side})
+    keep = pltpu.make_async_copy(slab(head), prompts.at[mine], lsem)
+    keep.start()
+
+    def spread(at, src, slot):
+        for other in range(1, share):
+            target = head * share + lax.rem(side + other, share)
+            send(src, slot, p2s.at[other, at], p2r.at[other, at], {"tensor": target})
+        send(src, slot, p3s.at[0, at], p3r.at[0, at], {"replica": 1 - copy_of})
+
+    def pass_on(at):
+        for other in range(1, share):
+            slot = slot_of(plane_of(at), lax.rem(side + share - other, share), copy_of)
+            arrive(slot, p2r.at[other, at])
+            send(prompts.at[slot], slot, p3s.at[other, at], p3r.at[other, at], {"replica": 1 - copy_of})
+
+    spread(0, slab(head), mine)
+
     loads = []
     chunks = slots // chunk
     for at in range(chunks):
@@ -155,12 +200,33 @@
         copy = pltpu.make_async_copy(cache_ref.at[:, rows], cache.at[:, rows], csem.at[at])
         copy.start()
         loads.append(copy)
-
-    barrier = pltpu.get_barrier_semaphore()
-    for off in range(1, size):
-        pl.semaphore_signal(barrier, inc=1, device_id={"tensor": lax.rem(rank + off, size)}, device_id_type=MESH)
-    pl.semaphore_signal(barrier, inc=1, device_id={"replica": 1 - copy_of}, device_id_type=MESH)
-    pl.semaphore_wait(barrier, size)
+    weights = load_out(size, w_ref, wbuf, wsem, out_ref.shape[1])
+
+    for copy in hidden_loads:
+        copy.wait()
+
+    def normalize(at, carry):
+        rows = pl.ds(pl.multiple_of(at * 16, 16), 16)
+        hidden = normed[rows, :].astype(jnp.float32)
+        scale = lax.rsqrt(jnp.mean(hidden * hidden, axis=1, keepdims=True) + EPSILON)
+        normed[rows, :] = (hidden * scale * gain_ref[...]).astype(jnp.bfloat16)
+        return carry
+
+    lax.fori_loop(0, normed.shape[0] // 16, normalize, 0)
+    query_sum[...] = jnp.zeros_like(query_sum)
+    part_sum[...] = jnp.zeros_like(part_sum)
+
+    def project_in(at, carry):
+        for copy in weight_loads(at):
+            copy.wait()
+        deep = pl.ds(pl.multiple_of(at * depth, depth), depth)
+        part = normed[:, deep]
+        query_sum[...] += jnp.dot(part, wq[deep, :], preferred_element_type=jnp.float32)
+        part_sum[...] += jnp.dot(part, wkv[deep, :], preferred_element_type=jnp.float32)
+        return carry
+
+    lax.fori_loop(0, qsem.shape[0], project_in, 0)
+    part_ref[...] = part_sum[...].astype(jnp.bfloat16)
 
     column = rank // pieces
     kind = column // kv_heads
@@ -181,47 +247,14 @@
         def _():
             pltpu.make_async_copy(part_ref, parts.at[kind, piece], kr.at[kind, piece]).start()
 
-    def slot_of(plane, side_at, replica_at):
-        return (plane * share + side_at) * 2 + replica_at
-
-    def arrive(slot, sem):
-        pltpu.make_async_copy(prompts.at[slot], prompts.at[slot], sem).wait()
-
-    sent = []
-
-    def send(src, slot, send_sem, recv_sem, device):
-        copy = pltpu.make_async_remote_copy(
-            src_ref=src, dst_ref=prompts.at[slot], send_sem=send_sem, recv_sem=recv_sem,
-            device_id=device, device_id_type=MESH)
-        copy.start()
-        sent.append(copy)
-
-    def plane_of(at):
-        return lax.rem(head + kv_heads - offsets[at], kv_heads)
-
-    def slab(which):
-        return prompt_ref.at[:, :, :, pl.ds(pl.multiple_of(which * HD, HD), HD)]
-
-    mine = slot_of(head, side, copy_of)
-    for at in range(1, kv_heads):
-        target = lax.rem(head + offsets[at], kv_heads)
-        send(slab(target), mine, p1s.at[at], p1r.at[at], {"tensor": target * share + side})
-    keep = pltpu.make_async_copy(slab(head), prompts.at[mine], lsem)
-    keep.start()
-
-    def spread(at, src, slot):
-        for other in range(1, share):
-            target = head * share + lax.rem(side + other, share)
-            send(src, slot, p2s.at[other, at], p2r.at[other, at], {"tensor": target})
-        send(src, slot, p3s.at[0, at], p3r.at[0, at], {"replica": 1 - copy_of})
-
-    def pass_on(at):
-        for other in range(1, share):
-            slot = slot_of(plane_of(at), lax.rem(side + share - other, share), copy_of)
-            arrive(slot, p2r.at[other, at])
-            send(prompts.at[slot], slot, p3s.at[other, at], p3r.at[other, at], {"replica": 1 - copy_of})
-
-    spread(0, slab(head), mine)
+    def turn(values):
+        turned = values * cosine_ref[rows_of, :] + pltpu.roll(values, HD // 2, 1) * sine_ref[rows_of, :]
+        return turned.astype(jnp.bfloat16).astype(jnp.float32)
+
+    for step in range(steps):
+        rows_of = pl.ds(step * slots, slots)
+        for at in range(local_heads):
+            query_ref[:, step * local_heads + at, :] = turn(query_sum[rows_of, pl.ds(at * HD, HD)])
 
     for which in range(2):
         for at in range(pieces):
@@ -230,8 +263,8 @@
         jnp.concatenate([parts[which, at] for at in range(pieces)], axis=1).astype(jnp.float32)
         for which in range(2)
     ]
-    turned = joined[0] * cosine_ref[...] + pltpu.roll(joined[0], HD // 2, 1) * sine_ref[...]
-    turned = turned.astype(jnp.bfloat16).astype(jnp.float32)
+    rows_of = slice(None)
+    turned = turn(joined[0])
     for step in range(steps):
         new_keys[step] = turned[step * slots:(step + 1) * slots]
         new_values[step] = joined[1][step * slots:(step + 1) * slots]
@@ -292,6 +325,7 @@
             heads_ref[pl.ds(step * slots, slots), pl.ds(at * HD, HD)] = cache_out[
                 :, step * local_heads + at, :].astype(jnp.bfloat16)
 
+    project_out(size, weights, heads_ref, out_ref, wbuf, own_sum, send1, recv1, send2, recv2, s1s, s1r, s2s, s2r)
     for copy in sent:
         copy.wait_send()
     for target, copy in part_copies:
@@ -300,40 +334,66 @@
             copy.wait_send()
 
 
-def attention(lengths, plengths, local_slot, request, matched, queries, part, cosine, sine, cache_kv, prompt_kv, size):
-    slots, head_rows, _ = queries.shape
-    rows, width = part.shape
-    steps = rows // slots
+def attention_block(
+    lengths, plengths, local_slot, request, matched, gain, cosine, sine,
+    hidden_in, w_query, w_keyval, cache_kv, prompt_kv, w_out, size,
+):
+    steps, slots, model_width = hidden_in.shape
+    rows = steps * slots
+    columns = w_query.shape[1]
+    head_rows = steps * columns // HD
+    width = w_keyval.shape[1]
+    share = size // (prompt_kv.shape[3] // HD)
     kv_heads = prompt_kv.shape[3] // HD
-    share = size // kv_heads
     requests = plengths.shape[0]
     senders = requests // prompt_kv.shape[1]
+    out_width = w_out.shape[1] // size
+    half = size // 2
+    splits = 8
     smem = pl.BlockSpec(memory_space=pltpu.SMEM)
     vmem = pl.BlockSpec(memory_space=pltpu.VMEM)
     hbm = pl.BlockSpec(memory_space=pl.ANY)
     dma = pltpu.SemaphoreType.DMA
     return pl.pallas_call(
-        functools.partial(attend_kernel, size),
-        out_shape=jax.ShapeDtypeStruct((rows, head_rows // steps * HD), jnp.bfloat16),
-        in_specs=[smem] * 5 + [vmem] * 4 + [hbm] * 2,
+        functools.partial(whole_kernel, size),
+        out_shape=jax.ShapeDtypeStruct((rows, out_width), jnp.bfloat16),
+        in_specs=[smem] * 5 + [vmem] * 3 + [hbm] * 6,
         out_specs=vmem,
         scratch_shapes=[
+            pltpu.VMEM((rows, model_width), jnp.bfloat16),
+            pltpu.VMEM(w_query.shape, jnp.bfloat16),
+            pltpu.VMEM(w_keyval.shape, jnp.bfloat16),
+            pltpu.VMEM((rows, columns), jnp.float32),
+            pltpu.VMEM((rows, width), jnp.float32),
+            pltpu.VMEM((rows, width), jnp.bfloat16),
+            pltpu.VMEM((slots, head_rows, HD), jnp.float32),
+            pltpu.VMEM((rows, columns), jnp.bfloat16),
             pltpu.VMEM(cache_kv.shape, jnp.bfloat16),
             pltpu.VMEM((senders, 2, prompt_kv.shape[1], prompt_kv.shape[2], HD), jnp.bfloat16),
             pltpu.VMEM((2, HD // width, rows, width), jnp.bfloat16),
             pltpu.VMEM((steps, slots, HD), jnp.float32),
             pltpu.VMEM((steps, slots, HD), jnp.float32),
-            pltpu.VMEM(queries.shape, jnp.float32),
+            pltpu.VMEM((slots, head_rows, HD), jnp.float32),
             pltpu.VMEM((requests, head_rows, HD), jnp.float32),
+            pltpu.VMEM((half, 2, columns, out_width), jnp.bfloat16),
+            pltpu.VMEM((half, rows, out_width), jnp.float32),
+            pltpu.VMEM((half, rows, out_width), jnp.bfloat16),
+            pltpu.VMEM((half, rows, out_width), jnp.bfloat16),
+            pltpu.VMEM((half - 1, rows, out_width), jnp.bfloat16),
+            pltpu.VMEM((half - 1, rows, out_width), jnp.bfloat16),
+            dma((steps,)), dma((splits,)), dma((splits,)),
             dma((slots // 8,)),
             dma,
             dma((kv_heads,)), dma((kv_heads,)),
             dma((share, kv_heads)), dma((share, kv_heads)),
             dma((share, kv_heads)), dma((share, kv_heads)),
             dma((share,)), dma((2, HD // width)),
+            dma((half, 2)), dma((half,)), dma((half,)), dma((half - 1,)), dma((half - 1,)),
         ],
-        compiler_params=pltpu.CompilerParams(collective_id=2, has_side_effects=True, vmem_limit_bytes=48 * 2**20),
-    )(lengths, plengths, local_slot, request, matched, queries, part, cosine, sine, cache_kv, prompt_kv)
+        compiler_params=pltpu.CompilerParams(collective_id=1, has_side_effects=True, vmem_limit_bytes=56 * 2**20),
+    )(lengths, plengths, local_slot, request, matched, gain, cosine, sine,
+      hidden_in, w_query, w_keyval, cache_kv, prompt_kv, w_out)
+
 
 def local(
     hidden_in,
@@ -350,15 +410,6 @@
     tensor_size = lax.axis_size("tensor")
     replica_rank = lax.axis_index("replica")
     step_count, row_count, model_width = hidden_in.shape
-    local_heads = w_query.shape[1] // HD
-    hidden = hidden_in.astype(jnp.float32)
-    scale = lax.rsqrt(jnp.mean(hidden * hidden, -1, keepdims=True) + EPSILON)
-    normed = (hidden * scale * norm_gain.astype(jnp.float32)).astype(jnp.bfloat16)
-    flat = normed.reshape(step_count * row_count, model_width)
-    queries = jnp.dot(flat, w_query, preferred_element_type=jnp.float32).reshape(
-        step_count, row_count, local_heads, HD
-    )
-    keyval_part = jnp.dot(flat, w_keyval, preferred_element_type=jnp.float32).astype(jnp.bfloat16)
     slot_ids = replica_rank * row_count + jnp.arange(row_count, dtype=jnp.int32)
     matches = slot_of[None, :] == slot_ids[:, None]
     matched = jnp.any(matches, 1)
@@ -374,26 +425,24 @@
     sine = jnp.sin(angles)
     cosine = jnp.concatenate([cosine, cosine], -1)
     sine = jnp.concatenate([-sine, sine], -1)
-    swapped = jnp.concatenate([queries[..., half_dim:], queries[..., :half_dim]], -1)
-    queries = queries * cosine[:, :, None] + swapped * sine[:, :, None]
-    queries = queries.astype(jnp.bfloat16).astype(jnp.float32)
-    queries = queries.transpose(1, 0, 2, 3).reshape(row_count, step_count * local_heads, HD)
     local_slot = jnp.clip(slot_of - replica_rank * row_count, 0, row_count - 1)
-    heads_flat = attention(
+    mixed = attention_block(
         cache_len,
         block_count * BLOCK,
         local_slot,
         request,
         matched.astype(jnp.int32),
-        queries,
-        keyval_part,
+        norm_gain.astype(jnp.float32)[None, :],
         cosine.reshape(step_count * row_count, HD),
         sine.reshape(step_count * row_count, HD),
+        hidden_in,
+        w_query,
+        w_keyval,
         cache_kv,
         prompt_kv,
+        w_out,
         tensor_size,
     )
-    mixed = project_out(heads_flat, w_out, tensor_size)
     return mixed.reshape(step_count, row_count, -1)
 
 

time: 122 us -> 104 us (0.85)
  local copies, waits for them, and re-layouts: 16.1 us -> 1.85 us
  matrix products: 7.16 us -> 0 us
  Pallas kernels: 91.7 us -> 95.2 us
    dot_general x1 -> x0, local copies, waits for them, and re-layouts: 11.6 us -> none  [local(): jnp.dot(flat, w_query, preferred_element_type=jnp.float32)]
    dot_general x2 -> x0, matrix products: 7.16 us -> none  [the longest x1 6.42 us: local(): jnp.dot(flat, w_query, preferred_element_type=jnp.float32)]
    pallas_call x2 -> x1, Pallas kernels: 91.7 us -> 95.2 us  [attention_block(): pl.pallas_call(functools.partial(whole_kernel, size), out_shape=jax.Shape...]
    unnamed x13 -> x1, local copies, waits for them, and re-layouts: 4.11 us -> 1.67 us
    reduce_sum x1 -> x0, other arithmetic: 2.26 us -> none  [local(): scale = lax.rsqrt(jnp.mean(hidden * hidden, -1, keepdims=True) + EPSILON)]
    broadcast_in_dim x0 -> x1, other arithmetic: none -> 1.33 us  [local(): norm_gain.astype(jnp.float32)[None, :]]
where the time goes in v3:
time: 104 us
  Pallas kernels  95.2 us (92%)
  other arithmetic  6.89 us (7%)
  local copies, waits for them, and re-layouts  1.85 us (2%)
    pallas_call x1, Pallas kernels, attention_block(): pl.pallas_call(functools.partial(whole_kernel, size), out_shape=jax.Shape...  95.2 us

profile of v3, /device:TPU:0, one launch (start us, length us, event | category | flops | bytes accessed | tf_op | source)
XLA Modules:
  0.0 104.0 jit_solution(15758303175004658853)
XLA Ops:
  0.0 0.7 compare_reduce_fusion
  0.8 0.5 convert_element_type.12.matched_ref
  1.3 1.3 %fusion.2 = (s32[64]{0:T(128)S(1)}, s32[64]{0:T(128)}) fusion(s32[32]{0:T(128)} %param.18, s32[64]{0:T(128)S(1)} %iota_add_fusion, s32[32]{0:T(128)} %param.19), kind=kLoop, calls=%fused_computation.9 | loop fusion | flops 10112 | bytes 1024 | tf_op jit(solution)/shard_map/reduce_sum | solution.py:418
  2.6 0.7 multiply_select_fusion
  3.3 0.1 add.34
  3.4 1.2 %subtract_clamp_fusion = (s32[32]{0:T(128)}, s32[32]{0:T(128)}) fusion(s32[32]{0:T(128)} %param.19, s32[]{:T(128)S(6)} %mul.38, s32[32]{0:T(128)} %param.18), kind=kLoop, calls=%fused_computation.14 | loop fusion | flops 96 | bytes 516 | tf_op jit(solution)/shard_map/jit(clip)/min | solution.py:428
  4.6 0.1 add.36
  4.7 1.3 %broadcast_in_dim.36 = f32[8192]{0:T(1024)} convert(bf16[8192]{0:T(1024)(128)(2,1)} %param.11) | non-fusion elementwise | flops 8192 | bytes 49152 | tf_op jit(solution)/shard_map/broadcast_in_dim | solution.py:435
  6.0 0.3 fusion
  6.3 0.7 pad_maximum_fusion
  7.1 95.2 %shard_map.100 = bf16[128,1024]{1,0:T(8,128)(2,1)} custom-call(s32[64]{0:T(128)} %length_ref.1, s32[32]{0:T(128)} %get-tuple-element.13.plength_ref, s32[32]{0:T(128)} %get-tuple-element.12.local_ref, s32[64]{0:T(128)} %get-tuple-element.6.request_ref, s32[64]{0:T(128)} %convert_element_type.12.matched_ref, f32[1,8192]{1,0:T(1,128)} %bitcast.5, ...), custom_call_target="tpu_custom_call" | custom-call | tf_op jit(solution)/shard_map/pallas_call | solution.py:357
  102.3 1.7 %copy.12 = bf16[2,64,1024]{2,1,0:T(8,128)(2,1)} copy(bf16[2,64,1024]{2,1,0:T(8,128)(2,1)} %bitcast.4) | data formatting | bytes 524288
  (5 shorter events, 0.0 us)

commit v4 on v3

--- a/solution.py
+++ b/solution.py
@@ -154,44 +154,58 @@
     def slot_of(plane, side_at, replica_at):
         return (plane * share + side_at) * 2 + replica_at
 
-    def arrive(slot, sem):
-        pltpu.make_async_copy(prompts.at[slot], prompts.at[slot], sem).wait()
+    def arrive(slot, which, sem):
+        pltpu.make_async_copy(prompts.at[slot, which], prompts.at[slot, which], sem).wait()
 
     sent = []
 
-    def send(src, slot, send_sem, recv_sem, device):
+    def send(src, slot, which, send_sem, recv_sem, device):
         copy = pltpu.make_async_remote_copy(
-            src_ref=src, dst_ref=prompts.at[slot], send_sem=send_sem, recv_sem=recv_sem,
+            src_ref=src, dst_ref=prompts.at[slot, which], send_sem=send_sem, recv_sem=recv_sem,
             device_id=device, device_id_type=MESH)
         copy.start()
-        sent.append(copy)
+        return copy
 
     def plane_of(at):
         return lax.rem(head + kv_heads - offsets[at], kv_heads)
 
-    def slab(which):
-        return prompt_ref.at[:, :, :, pl.ds(pl.multiple_of(which * HD, HD), HD)]
+    def slab(plane, which):
+        return prompt_ref.at[which, :, :, pl.ds(pl.multiple_of(plane * HD, HD), HD)]
 
     mine = slot_of(head, side, copy_of)
-    for at in range(1, kv_heads):
-        target = lax.rem(head + offsets[at], kv_heads)
-        send(slab(target), mine, p1s.at[at], p1r.at[at], {"tensor": target * share + side})
-    keep = pltpu.make_async_copy(slab(head), prompts.at[mine], lsem)
-    keep.start()
-
-    def spread(at, src, slot):
+    turns = [(at, which) for at in range(1, kv_heads) for which in range(2)]
+    outgoing = []
+
+    def send_next():
+        if len(outgoing) < len(turns):
+            at, which = turns[len(outgoing)]
+            target = lax.rem(head + offsets[at], kv_heads)
+            outgoing.append(send(
+                slab(target, which), mine, which, p1s.at[at, which], p1r.at[at, which],
+                {"tensor": target * share + side}))
+
+    def spread(at, which, src, slot):
         for other in range(1, share):
             target = head * share + lax.rem(side + other, share)
-            send(src, slot, p2s.at[other, at], p2r.at[other, at], {"tensor": target})
-        send(src, slot, p3s.at[0, at], p3r.at[0, at], {"replica": 1 - copy_of})
-
-    def pass_on(at):
+            sent.append(send(
+                src, slot, which, p2s.at[other, at, which], p2r.at[other, at, which], {"tensor": target}))
+        sent.append(send(src, slot, which, p3s.at[0, at, which], p3r.at[0, at, which], {"replica": 1 - copy_of}))
+
+    def pass_on(at, which):
         for other in range(1, share):
             slot = slot_of(plane_of(at), lax.rem(side + share - other, share), copy_of)
-            arrive(slot, p2r.at[other, at])
-            send(prompts.at[slot], slot, p3s.at[other, at], p3r.at[other, at], {"replica": 1 - copy_of})
-
-    spread(0, slab(head), mine)
+            arrive(slot, which, p2r.at[other, at, which])
+            sent.append(send(
+                prompts.at[slot, which], slot, which, p3s.at[other, at, which], p3r.at[other, at, which],
+                {"replica": 1 - copy_of}))
+
+    send_next()
+    send_next()
+    for which in range(2):
+        spread(0, which, slab(head, which), mine)
+    keeps = [pltpu.make_async_copy(slab(head, which), prompts.at[mine, which], lsem.at[which]) for which in range(2)]
+    for keep in keeps:
+        keep.start()
 
     loads = []
     chunks = slots // chunk
@@ -281,29 +295,19 @@
                 query_ref[slot], cache[0, slot], cache[1, slot], length_ref[slot], keys, values, local_heads)
         return carry
 
-    groups = kv_heads
-    each = chunks // groups
-    for group in range(groups):
-        if group + 1 < kv_heads:
-            slot = slot_of(plane_of(group + 1), side, copy_of)
-            arrive(slot, p1r.at[group + 1])
-            spread(group + 1, prompts.at[slot], slot)
-        pass_on(group)
-        for at in range(group * each, (group + 1) * each):
-            loads[at].wait()
-        lax.fori_loop(group * each, (group + 1) * each, cache_chunk, 0)
-
-    keep.wait()
     per_plane = share * 2 * per_device
     batch = min(8, per_plane)
-    for group in range(kv_heads):
-        plane = plane_of(group)
-        for other in range(share):
-            arrive(slot_of(plane, lax.rem(side + share - other, share), 1 - copy_of), p3r.at[other, group])
-
-        def prompt_chunk(at, carry, plane=plane):
+
+    def prompt_plane(at):
+        plane = plane_of(at)
+        for which in range(2):
+            for other in range(share):
+                slot = slot_of(plane, lax.rem(side + share - other, share), 1 - copy_of)
+                arrive(slot, which, p3r.at[other, at, which])
+
+        def prompt_chunk(step, carry):
             for inner in range(batch):
-                sender = plane * (share * 2) + at * (batch // per_device) + inner // per_device
+                sender = plane * (share * 2) + step * (batch // per_device) + inner // per_device
                 within = inner % per_device
                 request = sender * per_device + within
                 slot = local_ref[request]
@@ -314,6 +318,32 @@
             return carry
 
         lax.fori_loop(0, per_plane // batch, prompt_chunk, 0)
+
+    waiting = [(0, 0), (0, 1)]
+    done = 0
+    for step, (at, which) in enumerate(turns):
+        slot = slot_of(plane_of(at), side, copy_of)
+        arrive(slot, which, p1r.at[at, which])
+        outgoing[step].wait_send()
+        send_next()
+        spread(at, which, prompts.at[slot, which], slot)
+        if step == 0:
+            pass_on(*waiting.pop(0))
+        pass_on(*waiting.pop(0))
+        waiting.append((at, which))
+        upto = min(chunks, -(-chunks * (step + 1) // len(turns)))
+        for number in range(done, upto):
+            loads[number].wait()
+        lax.fori_loop(done, upto, cache_chunk, 0)
+        done = upto
+        if which == 1:
+            if at == 1:
+                for keep in keeps:
+                    keep.wait()
+            prompt_plane(at - 1)
+    for late in waiting:
+        pass_on(*late)
+    prompt_plane(kv_heads - 1)
 
     def choose(slot, carry):
         cache_out[slot] = jnp.where(matched_ref[slot] > 0, prompt_out[request_ref[slot]], cache_out[slot])
@@ -383,10 +413,10 @@
             pltpu.VMEM((half - 1, rows, out_width), jnp.bfloat16),
             dma((steps,)), dma((splits,)), dma((splits,)),
             dma((slots // 8,)),
-            dma,
-            dma((kv_heads,)), dma((kv_heads,)),
-            dma((share, kv_heads)), dma((share, kv_heads)),
-            dma((share, kv_heads)), dma((share, kv_heads)),
+            dma((2,)),
+            dma((kv_heads, 2)), dma((kv_heads, 2)),
+            dma((share, kv_heads, 2)), dma((share, kv_heads, 2)),
+            dma((share, kv_heads, 2)), dma((share, kv_heads, 2)),
             dma((share,)), dma((2, HD // width)),
             dma((half, 2)), dma((half,)), dma((half,)), dma((half - 1,)), dma((half - 1,)),
         ],

time: 104 us -> 101 us (0.971)
  Pallas kernels: 95.2 us -> 91.3 us
    pallas_call x1, Pallas kernels: 95.2 us -> 91.3 us  [attention_block(): pl.pallas_call(functools.partial(whole_kernel, size), out_shape=jax.Shape...]
where the time goes in v4:
time: 101 us; the launch traced here: 100 us
  Pallas kernels  91.3 us (90%)
  other arithmetic  6.89 us (7%)
  local copies, waits for them, and re-layouts  1.85 us (2%)
    pallas_call x1, Pallas kernels, attention_block(): pl.pallas_call(functools.partial(whole_kernel, size), out_shape=jax.Shape...  91.3 us

profile of v4, /device:TPU:0, one launch (start us, length us, event | category | flops | bytes accessed | tf_op | source)
XLA Modules:
  0.0 100.0 jit_solution(2428744128034512904)
XLA Ops:
  0.0 0.7 compare_reduce_fusion
  0.8 0.5 convert_element_type.12.matched_ref
  1.3 1.3 %fusion.2 = (s32[64]{0:T(128)S(1)}, s32[64]{0:T(128)}) fusion(s32[32]{0:T(128)} %param.18, s32[64]{0:T(128)S(1)} %iota_add_fusion, s32[32]{0:T(128)} %param.19), kind=kLoop, calls=%fused_computation.9 | loop fusion | flops 10112 | bytes 1024 | tf_op jit(solution)/shard_map/reduce_sum | solution.py:448
  2.6 0.7 multiply_select_fusion
  3.3 0.1 add.34
  3.4 1.2 %subtract_clamp_fusion = (s32[32]{0:T(128)}, s32[32]{0:T(128)}) fusion(s32[32]{0:T(128)} %param.19, s32[]{:T(128)S(6)} %mul.38, s32[32]{0:T(128)} %param.18), kind=kLoop, calls=%fused_computation.14 | loop fusion | flops 96 | bytes 516 | tf_op jit(solution)/shard_map/jit(clip)/min | solution.py:458
  4.6 0.1 add.36
  4.7 1.3 %broadcast_in_dim.36 = f32[8192]{0:T(1024)} convert(bf16[8192]{0:T(1024)(128)(2,1)} %param.11) | non-fusion elementwise | flops 8192 | bytes 49152 | tf_op jit(solution)/shard_map/broadcast_in_dim | solution.py:465
  6.0 0.3 fusion
  6.3 0.7 pad_maximum_fusion
  7.1 91.3 %shard_map.100 = bf16[128,1024]{1,0:T(8,128)(2,1)} custom-call(s32[64]{0:T(128)} %length_ref.1, s32[32]{0:T(128)} %get-tuple-element.13.plength_ref, s32[32]{0:T(128)} %get-tuple-element.12.local_ref, s32[64]{0:T(128)} %get-tuple-element.6.request_ref, s32[64]{0:T(128)} %convert_element_type.12.matched_ref, f32[1,8192]{1,0:T(1,128)} %bitcast.5, ...), custom_call_target="tpu_custom_call" | custom-call | tf_op jit(solution)/shard_map/pallas_call | solution.py:387
  98.4 1.7 %copy.12 = bf16[2,64,1024]{2,1,0:T(8,128)(2,1)} copy(bf16[2,64,1024]{2,1,0:T(8,128)(2,1)} %bitcast.4) | data formatting | bytes 524288
  (5 shorter events, 0.0 us)
